TPU v7x, 32 devices: a whole 2x2x4 slice. The times are simulated.
32 devices in a mesh: ctx: 16 (over z, x, core), fsdp: 2 (over y).
Axes of the slice: x: 2, y: 2, z: 4, core: 2. Of those that a mesh axis runs over, the one named last changes fastest.
Arguments:
- inputs: bfloat16 [2, 2, 2048, 768], P(None, 'fsdp', 'ctx'), may hold values from -6 to 6
- cotangent: bfloat16 [2, 2, 2048, 768], P(None, 'fsdp', 'ctx'), may hold values from -6 to 6
- lengths: int32 [2, 2], P(None, 'fsdp'), may hold values from 512 to 2048, as said below
- ln1_gain: bfloat16 [768], P('fsdp'), may hold values from 0.5 to 1.5
- ln1_bias: bfloat16 [768], P('fsdp'), may hold values from -1.75 to 1.75
- w_qkv: bfloat16 [768, 2304], P('fsdp'), may hold values from -0.21875 to 0.21875
- bias_q: bfloat16 [768], P('fsdp'), may hold values from -1.75 to 1.75
- bias_v: bfloat16 [768], P('fsdp'), may hold values from -1.75 to 1.75
- w_out: bfloat16 [768, 768], P('fsdp'), may hold values from -2.5 to 2.5
- bias_out: bfloat16 [768], P('fsdp'), may hold values from -1.75 to 1.75
- ln2_gain: bfloat16 [768], P('fsdp'), may hold values from 0.5 to 1.5
- ln2_bias: bfloat16 [768], P('fsdp'), may hold values from -1.75 to 1.75
- w_up: bfloat16 [768, 3072], P('fsdp'), may hold values from -0.21875 to 0.21875
- bias_up: bfloat16 [3072], P('fsdp'), may hold values from -1.75 to 1.75
- w_down: bfloat16 [3072, 768], P('fsdp'), may hold values from -0.109375 to 0.109375
- bias_down: bfloat16 [768], P('fsdp'), may hold values from -1.75 to 1.75
Outputs:
- outputs: bfloat16 [2, 2, 2048, 768], P(None, 'fsdp', 'ctx')
- grad_inputs: bfloat16 [2, 2, 2048, 768], P(None, 'fsdp', 'ctx')
- grad_ln1_gain: float32 [768], P('fsdp')
- grad_ln1_bias: float32 [768], P('fsdp')
- grad_w_qkv: float32 [768, 2304], P('fsdp')
- grad_bias_q: float32 [768], P('fsdp')
- grad_bias_v: float32 [768], P('fsdp')
- grad_w_out: float32 [768, 768], P('fsdp')
- grad_bias_out: float32 [768], P('fsdp')
- grad_ln2_gain: float32 [768], P('fsdp')
- grad_ln2_bias: float32 [768], P('fsdp')
- grad_w_up: float32 [768, 3072], P('fsdp')
- grad_bias_up: float32 [3072], P('fsdp')
- grad_w_down: float32 [3072, 768], P('fsdp')
- grad_bias_down: float32 [768], P('fsdp')
Inputs may be any that keep to these rules, and one draw needn't show every extreme that they name: For each of the 2 sequence places, one of the 2 micro-batches, drawn from the seed, has length 2048; the other lengths are drawn evenly.
All inputs are finite; a program needn't handle non-finite values.
Results may differ from a plain program's by a relative error of at most 0.023.
Values may be sent and summed in bfloat16 or wider, within the bound.
A program may use at most 320 MiB of HBM per device.

v0:
```python
import jax
import jax.numpy as jnp
from jax import lax
from jax.sharding import PartitionSpec as P

HEADS = 12
HDIM = 64


epsilon = 1e-06
masked_score = -1e30


def for_sending(value):

    def short(part):
        return part.astype(jnp.bfloat16) if part.dtype == jnp.float32 else part

    return jax.tree.map(short, value)


def layer_norm(values, scaling, offset):
    row_mean = jnp.mean(values, axis=-1, keepdims=True)
    centred = values - row_mean
    variance = jnp.mean(centred * centred, axis=-1, keepdims=True)
    return centred * lax.rsqrt(variance + epsilon) * scaling + offset


def gelu_exact(values):
    return jax.nn.gelu(values, approximate=False)


def split_heads(matrix):
    return matrix.reshape(matrix.shape[0], HEADS, matrix.shape[1] // HEADS)


def pair_scores(query_rows, key_rows):
    raw_scores = jnp.einsum(
        "qhd,khd->hqk",
        split_heads(query_rows),
        split_heads(key_rows),
        preferred_element_type=jnp.float32,
    )
    return raw_scores * HDIM ** (-0.5)


def body(
    inputs,
    cotangent,
    lengths,
    ln1_gain,
    ln1_bias,
    w_qkv,
    bias_q,
    bias_v,
    w_out,
    bias_out,
    ln2_gain,
    ln2_bias,
    w_up,
    bias_up,
    w_down,
    bias_down,
):
    local_rows = inputs.shape[2]
    model_width = inputs.shape[3]
    head_size = model_width // HEADS
    positions = lax.axis_index("ctx") * local_rows + jnp.arange(local_rows)
    totals = None
    output_list = []
    grad_list = []
    for micro_batch in range(inputs.shape[0]):
        gathered = (
            lax.all_gather(ln1_gain, "fsdp", axis=0, tiled=True),
            lax.all_gather(ln1_bias, "fsdp", axis=0, tiled=True),
            lax.all_gather(w_qkv, "fsdp", axis=0, tiled=True),
            lax.all_gather(bias_q, "fsdp", axis=0, tiled=True),
            lax.all_gather(bias_v, "fsdp", axis=0, tiled=True),
            lax.all_gather(w_out, "fsdp", axis=0, tiled=True),
            lax.all_gather(bias_out, "fsdp", axis=0, tiled=True),
            lax.all_gather(ln2_gain, "fsdp", axis=0, tiled=True),
            lax.all_gather(ln2_bias, "fsdp", axis=0, tiled=True),
            lax.all_gather(w_up, "fsdp", axis=0, tiled=True),
            lax.all_gather(bias_up, "fsdp", axis=0, tiled=True),
            lax.all_gather(w_down, "fsdp", axis=0, tiled=True),
            lax.all_gather(bias_down, "fsdp", axis=0, tiled=True),
        )
        (
            first_scale,
            first_shift,
            joint_full,
            query_shift,
            value_shift,
            output_full,
            output_shift,
            second_scale,
            second_shift,
            upward_full,
            upward_shift,
            downward_full,
            downward_shift,
        ) = gathered
        length = lengths[micro_batch, 0]
        source = inputs[micro_batch, 0].astype(jnp.float32)
        cot_rows = cotangent[micro_batch, 0].astype(jnp.float32)
        live_rows = positions < length
        normed_first, first_pull = jax.vjp(
            layer_norm, source, first_scale.astype(jnp.float32), first_shift.astype(jnp.float32)
        )
        first_low = normed_first.astype(jnp.bfloat16)
        shifts = jnp.concatenate([query_shift, jnp.zeros_like(query_shift), value_shift]).astype(
            jnp.float32
        )
        joint_rows = (
            jnp.dot(first_low, joint_full, preferred_element_type=jnp.float32) + shifts
        ).astype(jnp.bfloat16)
        queries = joint_rows[:, :model_width]
        key_rows = joint_rows[:, model_width : 2 * model_width]
        value_rows = joint_rows[:, 2 * model_width :]
        empty_rows = jnp.zeros((HEADS, local_rows), jnp.float32)
        run_max = empty_rows + masked_score
        run_sum = empty_rows
        run_acc = jnp.zeros((HEADS, local_rows, head_size), jnp.float32)
        piece_keys = lax.all_gather(key_rows, "ctx", axis=0, tiled=True)
        piece_values = lax.all_gather(value_rows, "ctx", axis=0, tiled=True)
        piece_rows = piece_keys.shape[0]
        live_keys = jnp.arange(piece_rows) < length
        scores = jnp.where(live_keys, pair_scores(queries, piece_keys), masked_score)
        new_max = jnp.maximum(run_max, jnp.max(scores, axis=-1))
        weights = jnp.where(live_keys, jnp.exp(scores - new_max[:, :, None]), 0.0)
        factor = jnp.exp(run_max - new_max)
        new_sum = run_sum * factor + jnp.sum(weights, axis=-1)
        update = jnp.einsum(
            "hqk,khd->hqd",
            weights.astype(jnp.bfloat16),
            split_heads(piece_values),
            preferred_element_type=jnp.float32,
        )
        run_max, run_sum, run_acc = (new_max, new_sum, run_acc * factor[:, :, None] + update)
        log_total = run_max + jnp.log(run_sum)
        attended = (
            (run_acc / run_sum[:, :, None]).transpose(1, 0, 2).reshape(local_rows, model_width)
        )
        attended_low = attended.astype(jnp.bfloat16)
        residual = (
            source
            + jnp.dot(attended_low, output_full, preferred_element_type=jnp.float32)
            + output_shift.astype(jnp.float32)
        )
        normed_second, second_pull = jax.vjp(
            layer_norm, residual, second_scale.astype(jnp.float32), second_shift.astype(jnp.float32)
        )
        second_low = normed_second.astype(jnp.bfloat16)
        upper = jnp.dot(
            second_low, upward_full, preferred_element_type=jnp.float32
        ) + upward_shift.astype(jnp.float32)
        active, gelu_pull = jax.vjp(gelu_exact, upper)
        active_low = active.astype(jnp.bfloat16)
        result = (
            residual
            + jnp.dot(active_low, downward_full, preferred_element_type=jnp.float32)
            + downward_shift.astype(jnp.float32)
        )
        output_list.append(result.astype(jnp.bfloat16))
        grad_out = jnp.where(live_rows[:, None], cot_rows, 0.0)
        grad_low = grad_out.astype(jnp.bfloat16)
        grad_down = jnp.einsum(
            "tf,td->fd", active_low, grad_low, preferred_element_type=jnp.float32
        )
        grad_down_shift = jnp.sum(grad_out, axis=0)
        grad_active = jnp.einsum(
            "td,fd->tf", grad_low, downward_full, preferred_element_type=jnp.float32
        )
        grad_upper = gelu_pull(grad_active)[0].astype(jnp.bfloat16)
        grad_up = jnp.einsum(
            "td,tf->df", second_low, grad_upper, preferred_element_type=jnp.float32
        )
        grad_up_shift = jnp.sum(grad_upper.astype(jnp.float32), axis=0)
        grad_second = jnp.einsum(
            "tf,df->td", grad_upper, upward_full, preferred_element_type=jnp.float32
        )
        grad_resid, grad_second_scale, grad_second_shift = second_pull(grad_second)
        grad_resid = grad_resid + grad_out
        grad_branch = grad_resid.astype(jnp.bfloat16)
        grad_output = jnp.einsum(
            "tc,td->cd", attended_low, grad_branch, preferred_element_type=jnp.float32
        )
        grad_output_shift = jnp.sum(grad_branch.astype(jnp.float32), axis=0)
        grad_attended = jnp.einsum(
            "td,cd->tc", grad_branch, output_full, preferred_element_type=jnp.float32
        ).astype(jnp.bfloat16)
        row_delta = jnp.sum(
            (grad_attended.astype(jnp.float32) * attended).reshape(local_rows, HEADS, head_size),
            axis=-1,
        ).T
        back_piece_keys = lax.all_gather(key_rows, "ctx", axis=0, tiled=True)
        back_piece_values = lax.all_gather(value_rows, "ctx", axis=0, tiled=True)
        back_piece_rows = back_piece_keys.shape[0]
        back_live_keys = jnp.arange(back_piece_rows) < length
        probability = jnp.where(
            back_live_keys,
            jnp.exp(pair_scores(queries, back_piece_keys) - log_total[:, :, None]),
            0.0,
        )
        grad_prob = jnp.einsum(
            "qhd,khd->hqk",
            split_heads(grad_attended),
            split_heads(back_piece_values),
            preferred_element_type=jnp.float32,
        )
        dscore = (probability * (grad_prob - row_delta[:, :, None]) * HDIM ** (-0.5)).astype(
            jnp.bfloat16
        )
        grad_query = jnp.einsum(
            "hqk,khd->qhd", dscore, split_heads(back_piece_keys), preferred_element_type=jnp.float32
        ).reshape(local_rows, model_width)
        grad_key = jnp.einsum(
            "hqk,qhd->khd", dscore, split_heads(queries), preferred_element_type=jnp.float32
        ).reshape(back_piece_rows, model_width)
        grad_value = jnp.einsum(
            "hqk,qhd->khd",
            probability.astype(jnp.bfloat16),
            split_heads(grad_attended),
            preferred_element_type=jnp.float32,
        ).reshape(back_piece_rows, model_width)
        key_acc = grad_key
        value_acc = grad_value
        back_state = (grad_query, key_acc, value_acc)
        grad_query = back_state[0]
        grad_key, grad_value = (
            lax.psum_scatter(
                back_state[1].astype(jnp.bfloat16), "ctx", scatter_dimension=0, tiled=True
            ).astype(jnp.float32),
            lax.psum_scatter(
                back_state[2].astype(jnp.bfloat16), "ctx", scatter_dimension=0, tiled=True
            ).astype(jnp.float32),
        )
        grad_joint = jnp.concatenate(
            [
                grad_query.astype(jnp.bfloat16),
                grad_key.astype(jnp.bfloat16),
                grad_value.astype(jnp.bfloat16),
            ],
            axis=1,
        )
        grad_qkv = jnp.einsum(
            "td,tf->df", first_low, grad_joint, preferred_element_type=jnp.float32
        )
        grad_query_shift = jnp.sum(grad_joint[:, :model_width].astype(jnp.float32), axis=0)
        grad_value_shift = jnp.sum(grad_joint[:, 2 * model_width :].astype(jnp.float32), axis=0)
        grad_first = jnp.einsum(
            "tf,df->td", grad_joint, joint_full, preferred_element_type=jnp.float32
        )
        grad_source, grad_first_scale, grad_first_shift = first_pull(grad_first)
        grad_list.append((grad_source + grad_resid).astype(jnp.bfloat16))
        local_grads = (
            grad_first_scale,
            grad_first_shift,
            grad_qkv,
            grad_query_shift,
            grad_value_shift,
            grad_output,
            grad_output_shift,
            grad_second_scale,
            grad_second_shift,
            grad_up,
            grad_up_shift,
            grad_down,
            grad_down_shift,
        )
        shard_part = (
            lax.psum_scatter(
                local_grads[0].astype(jnp.bfloat16), "fsdp", scatter_dimension=0, tiled=True
            ).astype(jnp.float32),
            lax.psum_scatter(
                local_grads[1].astype(jnp.bfloat16), "fsdp", scatter_dimension=0, tiled=True
            ).astype(jnp.float32),
            lax.psum_scatter(
                local_grads[2].astype(jnp.bfloat16), "fsdp", scatter_dimension=0, tiled=True
            ).astype(jnp.float32),
            lax.psum_scatter(
                local_grads[3].astype(jnp.bfloat16), "fsdp", scatter_dimension=0, tiled=True
            ).astype(jnp.float32),
            lax.psum_scatter(
                local_grads[4].astype(jnp.bfloat16), "fsdp", scatter_dimension=0, tiled=True
            ).astype(jnp.float32),
            lax.psum_scatter(
                local_grads[5].astype(jnp.bfloat16), "fsdp", scatter_dimension=0, tiled=True
            ).astype(jnp.float32),
            lax.psum_scatter(
                local_grads[6].astype(jnp.bfloat16), "fsdp", scatter_dimension=0, tiled=True
            ).astype(jnp.float32),
            lax.psum_scatter(
                local_grads[7].astype(jnp.bfloat16), "fsdp", scatter_dimension=0, tiled=True
            ).astype(jnp.float32),
            lax.psum_scatter(
                local_grads[8].astype(jnp.bfloat16), "fsdp", scatter_dimension=0, tiled=True
            ).astype(jnp.float32),
            lax.psum_scatter(
                local_grads[9].astype(jnp.bfloat16), "fsdp", scatter_dimension=0, tiled=True
            ).astype(jnp.float32),
            lax.psum_scatter(
                local_grads[10].astype(jnp.bfloat16), "fsdp", scatter_dimension=0, tiled=True
            ).astype(jnp.float32),
            lax.psum_scatter(
                local_grads[11].astype(jnp.bfloat16), "fsdp", scatter_dimension=0, tiled=True
            ).astype(jnp.float32),
            lax.psum_scatter(
                local_grads[12].astype(jnp.bfloat16), "fsdp", scatter_dimension=0, tiled=True
            ).astype(jnp.float32),
        )
        totals = shard_part if totals is None else jax.tree.map(jnp.add, totals, shard_part)
    totals = jax.tree.map(
        lambda part: part.astype(jnp.float32), lax.psum(for_sending(totals), "ctx")
    )
    outputs = jnp.stack(output_list)[:, None]
    grad_inputs = jnp.stack(grad_list)[:, None]
    return (
        outputs,
        grad_inputs,
        totals[0],
        totals[1],
        totals[2],
        totals[3],
        totals[4],
        totals[5],
        totals[6],
        totals[7],
        totals[8],
        totals[9],
        totals[10],
        totals[11],
        totals[12],
    )


def solution(mesh):
    return jax.shard_map(
        body,
        mesh=mesh,
        in_specs=(
            P(None, "fsdp", "ctx", None),
            P(None, "fsdp", "ctx", None),
            P(None, "fsdp"),
            P("fsdp"),
            P("fsdp"),
            P("fsdp", None),
            P("fsdp"),
            P("fsdp"),
            P("fsdp", None),
            P("fsdp"),
            P("fsdp"),
            P("fsdp"),
            P("fsdp", None),
            P("fsdp"),
            P("fsdp", None),
            P("fsdp"),
        ),
        out_specs=(
            P(None, "fsdp", "ctx", None),
            P(None, "fsdp", "ctx", None),
            P("fsdp"),
            P("fsdp"),
            P("fsdp", None),
            P("fsdp"),
            P("fsdp"),
            P("fsdp", None),
            P("fsdp"),
            P("fsdp"),
            P("fsdp"),
            P("fsdp", None),
            P("fsdp"),
            P("fsdp", None),
            P("fsdp"),
        ),
        check_vma=False,
    )
```

profile of v0, /device:TPU:3, one launch (start us, length us, event | category | flops | bytes accessed | tf_op | source)
XLA Modules:
  0.0 1280.0 jit_solution(10556208058007939629)
XLA Ops:
  21.5 38.8 %all-gather.18.cloned.1.call-done = bf16[768,2304]{1,0:T(8,128)(2,1)} async-done(((bf16[384,2304]{1,0:T(8,128)(2,1)}), bf16[768,2304]{1,0:T(8,128)(2,1)}) %all-gather.18.cloned.1.call-update) | async-done | bytes 3538960 | tf_op jit(solution)/shard_map/all_gather | solution.py:76
  92.5 16.4 %all-gather.30.cloned.1.call-done = bf16[2048,768]{1,0:T(8,128)(2,1)} async-done(((bf16[128,768]{1,0:T(8,128)(2,1)}), bf16[2048,768]{1,0:T(8,128)(2,1)}) %all-gather.30.cloned.1.call-update) | async-done | bytes 3145744 | tf_op jit(solution)/shard_map/all_gather | solution.py:124
  121.2 34.8 %all-gather.20.cloned.1.call-done = bf16[2048,768]{1,0:T(8,128)(2,1)} async-done(((bf16[128,768]{1,0:T(8,128)(2,1)}), bf16[2048,768]{1,0:T(8,128)(2,1)}) %all-gather.20.cloned.1.call-update) | async-done | bytes 3145744 | tf_op jit(solution)/shard_map/all_gather | solution.py:124
  167.9 35.1 %all-gather.32.cloned.1.call-done = bf16[2048,768]{1,0:T(8,128)(2,1)} async-done(((bf16[128,768]{1,0:T(8,128)(2,1)}), bf16[2048,768]{1,0:T(8,128)(2,1)}) %all-gather.32.cloned.1.call-update) | async-done | bytes 3145744 | tf_op jit(solution)/shard_map/all_gather | solution.py:125
  207.6 10.1 fusion.67
  229.7 44.2 %all-gather.22.cloned.1.call-done = bf16[2048,768]{1,0:T(8,128)(2,1)} async-done(((bf16[128,768]{1,0:T(8,128)(2,1)}), bf16[2048,768]{1,0:T(8,128)(2,1)}) %all-gather.22.cloned.1.call-update) | async-done | bytes 3145744 | tf_op jit(solution)/shard_map/all_gather | solution.py:125
  278.8 10.3 fusion.64
  291.7 45.7 %all-gather.26.cloned.1.call-done = bf16[768,3072]{1,0:T(8,128)(2,1)} async-done(((bf16[384,3072]{1,0:T(8,128)(2,1)}), bf16[768,3072]{1,0:T(8,128)(2,1)}) %all-gather.26.cloned.1.call-update) | async-done | bytes 4718608 | tf_op jit(solution)/shard_map/all_gather | solution.py:83
  352.9 48.8 %all-gather.28.cloned.1.call-done = bf16[3072,768]{1,0:T(8,128)(2,1)} async-done(((bf16[1536,768]{1,0:T(8,128)(2,1)}), bf16[3072,768]{1,0:T(8,128)(2,1)}) %all-gather.28.cloned.1.call-update) | async-done | bytes 4718608 | tf_op jit(solution)/shard_map/all_gather | solution.py:85
  437.8 10.7 multiply_convert_fusion
  480.9 10.4 multiply_convert_fusion.1
  534.1 32.9 %reduce-scatter.41.cloned.1.call-done = bf16[128,768]{1,0:T(8,128)(2,1)} async-done(((bf16[2048,768]{1,0:T(8,128)(2,1)}), bf16[128,768]{1,0:T(8,128)(2,1)}) %reduce-scatter.41.cloned.1.call-update) | async-done | bytes 196624
  579.3 56.7 %reduce-scatter.39.cloned.1.call-done = bf16[128,768]{1,0:T(8,128)(2,1)} async-done(((bf16[2048,768]{1,0:T(8,128)(2,1)}), bf16[128,768]{1,0:T(8,128)(2,1)}) %reduce-scatter.39.cloned.1.call-update) | async-done | bytes 196624
  637.1 67.8 %reduce-scatter.37.cloned.1.call-done = bf16[128,768]{1,0:T(8,128)(2,1)} async-done(((bf16[2048,768]{1,0:T(8,128)(2,1)}), bf16[128,768]{1,0:T(8,128)(2,1)}) %reduce-scatter.37.cloned.1.call-update) | async-done | bytes 196624
  719.1 11.7 reduce-scatter.27.cloned.1.call-done
  730.8 24.0 %reduce-scatter.25.cloned.1.call-done = bf16[384,768]{1,0:T(8,128)(2,1)} async-done(((bf16[768,768]{1,0:T(8,128)(2,1)}), bf16[384,768]{1,0:T(8,128)(2,1)}) %reduce-scatter.25.cloned.1.call-update) | async-done | bytes 589840 | tf_op jit(solution)/shard_map/reduce_scatter | solution.py:287
  757.0 60.0 %reduce-scatter.35.cloned.1.call-done = bf16[1536,768]{1,0:T(8,128)(2,1)} async-done(((bf16[3072,768]{1,0:T(8,128)(2,1)}), bf16[1536,768]{1,0:T(8,128)(2,1)}) %reduce-scatter.35.cloned.1.call-update) | async-done | bytes 2359312 | tf_op jit(solution)/shard_map/reduce_scatter | solution.py:305
  817.0 62.3 %reduce-scatter.33.cloned.1.call-done = bf16[1536,768]{1,0:T(8,128)(2,1)} async-done(((bf16[3072,768]{1,0:T(8,128)(2,1)}), bf16[1536,768]{1,0:T(8,128)(2,1)}) %reduce-scatter.33.cloned.1.call-update) | async-done | bytes 2359312 | tf_op jit(solution)/shard_map/reduce_scatter | solution.py:305
  883.6 58.4 %reduce-scatter.31.cloned.1.call-done = bf16[384,3072]{1,0:T(8,128)(2,1)} async-done(((bf16[768,3072]{1,0:T(8,128)(2,1)}), bf16[384,3072]{1,0:T(8,128)(2,1)}) %reduce-scatter.31.cloned.1.call-update) | async-done | bytes 2359312 | tf_op jit(solution)/shard_map/reduce_scatter | solution.py:299
  942.0 62.9 %reduce-scatter.29.cloned.1.call-done = bf16[384,3072]{1,0:T(8,128)(2,1)} async-done(((bf16[768,3072]{1,0:T(8,128)(2,1)}), bf16[384,3072]{1,0:T(8,128)(2,1)}) %reduce-scatter.29.cloned.1.call-update) | async-done | bytes 2359312 | tf_op jit(solution)/shard_map/reduce_scatter | solution.py:299
  1009.5 45.9 %reduce-scatter.23.cloned.1.call-done = bf16[384,2304]{1,0:T(8,128)(2,1)} async-done(((bf16[768,2304]{1,0:T(8,128)(2,1)}), bf16[384,2304]{1,0:T(8,128)(2,1)}) %reduce-scatter.23.cloned.1.call-update) | async-done | bytes 1769488 | tf_op jit(solution)/shard_map/reduce_scatter | solution.py:278
  1055.4 49.9 %reduce-scatter.21.cloned.1.call-done = bf16[384,2304]{1,0:T(8,128)(2,1)} async-done(((bf16[768,2304]{1,0:T(8,128)(2,1)}), bf16[384,2304]{1,0:T(8,128)(2,1)}) %reduce-scatter.21.cloned.1.call-update) | async-done | bytes 1769488 | tf_op jit(solution)/shard_map/reduce_scatter | solution.py:278
  1128.0 54.7 %all-reduce.18 = (bf16[384]{0:T(512)(128)(2,1)S(1)}, bf16[384]{0:T(512)(128)(2,1)S(1)}, bf16[384]{0:T(512)(128)(2,1)S(1)}, bf16[384]{0:T(512)(128)(2,1)S(1)}, bf...) all-reduce(bf16[384]{0:T(512)(128)(2,1)S(1)} %add_convert_fusion.18, ...), channel_id=1, replica_groups=mesh['ctx'=16,'fsdp'=2] {'ctx'}, use_global_device_ids=true, to_apply=%region_30.31 | all-reduce | flops 4608 | bytes 18432 | tf_op jit(solution)/shard_map/psum | solution.py:314
  1189.0 73.7 %all-reduce.23.cloned.1.call-done = (bf16[384,2304]{1,0:T(8,128)(2,1)}, bf16[384,768]{1,0:T(8,128)(2,1)}, bf16[384,3072]{1,0:T(8,128)(2,1)}, bf16[1536,768]{1,0:T(8,128)(2,1)}) async-done(((bf16[384,2304]{1,0:T(8,128)(2,1)}, bf16[384,768]{1,0:T(8,128)(2,1)}, bf16[384,3072]{1,0:T(8,128)(2,1)}, bf16[1536,768]{1,0:T(8,128)(2,1)}), (bf16[384,2304]{1,0:T(8,128)(2,1)}, bf16[384,768]{1,0:T(8,128)(2,1)}, ...) | async-done | bytes 7077904 | tf_op jit(solution)/shard_map/psum | solution.py:314
  (418 shorter events, 296.6 us)
Async XLA Ops:
  7.2 53.0 %all-gather.18.cloned.1.call-start = ((), (), s32[]{:S(2)}) async-start(), calls=%async_computation.12 | async-start | bytes 5308416 | tf_op jit(solution)/shard_map/all_gather | solution.py:76
  8.0 100.9 %all-gather.30.cloned.1.call-start = ((), (), s32[]{:S(2)}) async-start(), calls=%async_computation.18 | async-start | bytes 3342336 | tf_op jit(solution)/shard_map/all_gather | solution.py:124
  63.8 92.2 %all-gather.20.cloned.1.call-start = ((), (), s32[]{:S(2)}) async-start(), calls=%async_computation.13 | async-start | bytes 3342336 | tf_op jit(solution)/shard_map/all_gather | solution.py:124
  67.4 135.6 %all-gather.32.cloned.1.call-start = ((), (), s32[]{:S(2)}) async-start(), calls=%async_computation.19 | async-start | bytes 3342336 | tf_op jit(solution)/shard_map/all_gather | solution.py:125
  68.0 158.5 %all-gather.24.cloned.1.call-start = ((), (), s32[]{:S(2)}) async-start(), calls=%async_computation.15 | async-start | bytes 1769472 | tf_op jit(solution)/shard_map/all_gather | solution.py:79
  68.5 205.3 %all-gather.22.cloned.1.call-start = ((), (), s32[]{:S(2)}) async-start(), calls=%async_computation.14 | async-start | bytes 3342336 | tf_op jit(solution)/shard_map/all_gather | solution.py:125
  69.1 268.3 %all-gather.26.cloned.1.call-start = ((), (), s32[]{:S(2)}) async-start(), calls=%async_computation.16 | async-start | bytes 7077888 | tf_op jit(solution)/shard_map/all_gather | solution.py:83
  69.9 331.7 %all-gather.28.cloned.1.call-start = ((), (), s32[]{:S(2)}) async-start(), calls=%async_computation.17 | async-start | bytes 7077888 | tf_op jit(solution)/shard_map/all_gather | solution.py:85
  70.7 461.7 %reduce-scatter.43.cloned.1.call-start = ((), (), s32[]{:S(2)}) async-start(), calls=%async_computation.31 | async-start | bytes 3342336
  434.0 132.9 %reduce-scatter.41.cloned.1.call-start = ((), (), s32[]{:S(2)}) async-start(), calls=%async_computation.30 | async-start | bytes 3342336
  456.9 179.1 %reduce-scatter.39.cloned.1.call-start = ((), (), s32[]{:S(2)}) async-start(), calls=%async_computation.29 | async-start | bytes 3342336
  477.0 227.8 %reduce-scatter.37.cloned.1.call-start = ((), (), s32[]{:S(2)}) async-start(), calls=%async_computation.28 | async-start | bytes 3342336
  499.5 231.3 %reduce-scatter.27.cloned.1.call-start = ((), (), s32[]{:S(2)}) async-start(), calls=%async_computation.23 | async-start | bytes 1769472 | tf_op jit(solution)/shard_map/reduce_scatter | solution.py:287
  502.1 252.6 %reduce-scatter.25.cloned.1.call-start = ((), (), s32[]{:S(2)}) async-start(), calls=%async_computation.22 | async-start | bytes 1769472 | tf_op jit(solution)/shard_map/reduce_scatter | solution.py:287
  504.7 312.2 %reduce-scatter.35.cloned.1.call-start = ((), (), s32[]{:S(2)}) async-start(), calls=%async_computation.27 | async-start | bytes 7077888 | tf_op jit(solution)/shard_map/reduce_scatter | solution.py:305
  509.7 369.6 %reduce-scatter.33.cloned.1.call-start = ((), (), s32[]{:S(2)}) async-start(), calls=%async_computation.26 | async-start | bytes 7077888 | tf_op jit(solution)/shard_map/reduce_scatter | solution.py:305
  514.6 427.5 %reduce-scatter.31.cloned.1.call-start = ((), (), s32[]{:S(2)}) async-start(), calls=%async_computation.25 | async-start | bytes 7077888 | tf_op jit(solution)/shard_map/reduce_scatter | solution.py:299
  519.6 485.2 %reduce-scatter.29.cloned.1.call-start = ((), (), s32[]{:S(2)}) async-start(), calls=%async_computation.24 | async-start | bytes 7077888 | tf_op jit(solution)/shard_map/reduce_scatter | solution.py:299
  525.0 530.4 %reduce-scatter.23.cloned.1.call-start = ((), (), s32[]{:S(2)}) async-start(), calls=%async_computation.21 | async-start | bytes 5308416 | tf_op jit(solution)/shard_map/reduce_scatter | solution.py:278
  572.9 133.1 %copy-start.51 = (f32[128]{0:T(128)S(1)}, f32[128]{0:T(128)}, u32[]{:S(2)}) copy-start(f32[128]{0:T(128)} %copy-done.50) | copy-start | bytes 1540
  572.9 532.4 %reduce-scatter.21.cloned.1.call-start = ((), (), s32[]{:S(2)}) async-start(), calls=%async_computation.20 | async-start | bytes 5308416 | tf_op jit(solution)/shard_map/reduce_scatter | solution.py:278
  709.9 552.7 %all-reduce.23.cloned.1.call-start = ((), (), s32[]{:S(2)}) async-start(), calls=%async_computation.32 | async-start | bytes 14155776 | tf_op jit(solution)/shard_map/psum | solution.py:314
  1120.0 67.9 %copy-start.25 = (f32[128,768]{1,0:T(8,128)S(1)}, f32[128,768]{1,0:T(8,128)}, u32[]{:S(2)}) copy-start(f32[128,768]{1,0:T(8,128)} %copy-done.24) | copy-start | bytes 1179652
  1120.1 67.9 %copy-start.84 = (f32[128]{0:T(128)S(1)}, f32[128]{0:T(128)}, u32[]{:S(2)}) copy-start(f32[128]{0:T(128)} %copy-done.83) | copy-start | bytes 1540
  (102 other events, 671.0 us)
Sparse Core Ops, SparseCore 0:
  9.6 50.5 all-gather.17
  63.9 44.9 all-gather.29
  111.7 44.2 all-gather.19
  158.7 44.2 all-gather.31
  204.3 22.0 all-gather.23
  229.2 44.6 all-gather.21
  275.4 61.9 all-gather.25
  339.0 62.6 all-gather.27
  434.2 63.8 reduce-scatter.42
  501.7 65.1 reduce-scatter.40
  570.8 65.1 reduce-scatter.38
  639.6 65.1 reduce-scatter.36
  707.7 23.0 reduce-scatter.26
  733.0 21.7 reduce-scatter.24
  756.9 59.9 reduce-scatter.34
  819.2 59.9 reduce-scatter.32
  882.0 59.9 reduce-scatter.30
  944.8 59.9 reduce-scatter.28
  1007.7 47.6 reduce-scatter.22
  1057.6 47.6 reduce-scatter.20
  1110.5 152.0 all-reduce.22
where the time goes:
time: 1290 us; the launch traced here: 1280 us
  waiting for transfers between devices  881 us (68%)
  matrix products  169 us (13%)
  blocking collectives  90.3 us (7%)
  local copies, waits for them, and re-layouts  65.8 us (5%)
  other arithmetic  55.7 us (4%)
  between operations  17.6 us (1%)
    unnamed x25, waiting for transfers between devices  161 us
    reduce_scatter x2, waiting for transfers between devices, body(): lax.psum_scatter(local_grads[11].astype(jnp.bfloat16), 'fsdp', scatter_di...  122 us
    reduce_scatter x2, waiting for transfers between devices, body(): lax.psum_scatter(local_grads[9].astype(jnp.bfloat16), 'fsdp', scatter_dim...  121 us
    reduce_scatter x2, waiting for transfers between devices, body(): lax.psum_scatter(local_grads[2].astype(jnp.bfloat16), 'fsdp', scatter_dim...  95.7 us
    all_gather x2, waiting for transfers between devices, body(): piece_values = lax.all_gather(value_rows, 'ctx', axis=0, tiled=True)  79.2 us
    psum x1, waiting for transfers between devices, body(): lax.psum(for_sending(totals), 'ctx')  73.7 us
    psum x1, blocking collectives, body(): lax.psum(for_sending(totals), 'ctx')  54.7 us
    all_gather x2, waiting for transfers between devices, body(): piece_keys = lax.all_gather(key_rows, 'ctx', axis=0, tiled=True)  51.2 us
  transfers between devices with their start and end apart: 21, of which 20 were waited for; matrix products, arithmetic and copies ran while one was open for 18% of the time, Pallas kernels for 0%

commit v1 on v0

v1 whole, which is shorter than its diff:
```python
import functools
import heapq

import jax
import jax.numpy as jnp
from jax import lax
from jax.experimental import pallas as pl
from jax.experimental.pallas import tpu as pltpu
from jax.sharding import PartitionSpec as P

HEADS = 12
HDIM = 64
GROUPS = 8
EPS = 1e-6
BF = jnp.bfloat16
F32 = jnp.float32
WIDE = 512
MESH = pl.DeviceIdType.MESH


def dot_nn(a, b):
    return lax.dot_general(a, b, (((1,), (0,)), ((), ())), preferred_element_type=F32)


def dot_nt(a, b):
    return lax.dot_general(a, b, (((1,), (1,)), ((), ())), preferred_element_type=F32)


def dot_tn(a, b):
    return lax.dot_general(a, b, (((0,), (0,)), ((), ())), preferred_element_type=F32)


def flip(index, bit):
    return index + bit - 2 * bit * ((index // bit) % 2)


def span(start, size, unit=16):
    return pl.ds(pl.multiple_of(start, unit), size)


class Copy:
    def __init__(self, wire, src, dst, ctx, fsdp, landing):
        self.wire, self.src, self.dst, self.landing = wire, src, dst, landing
        self.ctx, self.fsdp, self.i = ctx, fsdp, wire.count
        self.arrived = False
        wire.count += 1

    def of(self, dst):
        return pltpu.make_async_remote_copy(
            src_ref=self.src, dst_ref=dst, send_sem=self.wire.send.at[self.i], recv_sem=self.wire.recv.at[self.i],
            device_id=(self.ctx, self.fsdp), device_id_type=MESH,
        )

    def start(self):
        self.of(self.dst).start()
        self.wire.open.append(self)
        return self

    def arrive(self):
        self.of(self.landing).wait_recv()
        self.arrived = True

    def left(self):
        self.of(self.dst).wait_send()


class Wire:
    def __init__(self, send, recv, fsdp):
        self.send, self.recv, self.fsdp = send, recv, fsdp
        self.count, self.open = 0, []

    def copy(self, src, dst, ctx, fsdp=None, landing=None):
        return Copy(self, src, dst, ctx, self.fsdp if fsdp is None else fsdp, dst if landing is None else landing)

    def drain(self, copies=None):
        for copy in list(self.open) if copies is None else copies:
            copy.left()
            self.open.remove(copy)

    def finish(self):
        for copy in self.open:
            if not copy.arrived:
                copy.arrive()
        self.drain()


class Planner:
    def __init__(self):
        self.now, self.free, self.queue, self.serial = 0.0, {}, [], 0

    def ship(self, loads):
        end = self.now
        for link, us in loads.items():
            self.free[link] = max(self.now, self.free.get(link, 0.0)) + us
            end = max(end, self.free[link])
        return end + 1.5

    def later(self, when, run):
        self.serial += 1
        heapq.heappush(self.queue, (when, self.serial, run))

    def until(self, when):
        while self.queue and self.queue[0][0] <= max(self.now, when):
            at, _, run = heapq.heappop(self.queue)
            self.now = max(self.now, at)
            run()
            self.now += 0.2
        self.now = max(self.now, when)

    def compute(self, us, run, needs=0.0):
        self.until(needs)
        out = run()
        self.now += us
        return out

    def finish(self):
        self.until(1e9)


def road(axis, bit, us):
    if axis == "f":
        return {"y%d" % bit: us}
    return {1: {"core": us / 5}, 2: {"x": us}, 4: {"z": us}, 8: {"z": us, "mid": 2 * us}}.get(bit, {"far%d" % bit: us})


class Gather:
    def __init__(self, wire, c, f, nf, p, shard, full):
        rows = shard.shape[0]
        n = rows // p
        r = c % p
        self.a, self.b, self.z = [], [], []
        at = lambda owner, part: full.at[span(owner * rows + part * n, n)]
        sib = lambda i: flip(i, 1)
        for d in range(1, nf):
            fs = (f + nf - d) % nf
            self.a.append(wire.copy(shard.at[span(r * n, n)], at(f, r), c, (f + d) % nf, landing=at(fs, r)))
            near = []
            for j in range(1, p // 2):
                other, part = c, r
                for bit in (2, 4):
                    if (2 * j) & bit:
                        other, part = flip(other, bit), flip(part, bit)
                near.append((wire.copy(at(fs, r), at(fs, r), other, landing=at(fs, part)), part))
            self.b.append([copy for copy, _ in near])
            self.z.append([wire.copy(at(fs, q), at(fs, q), sib(c), landing=at(fs, sib(q))) for q in [r] + [q for _, q in near]])

    def begin(self):
        for copy in self.a:
            copy.start()

    def spread(self):
        for a, b, z in zip(self.a, self.b, self.z):
            a.arrive()
            for copy in b:
                copy.start()
            z[0].start()

    def pass_on(self):
        for b, z in zip(self.b, self.z):
            for near, sib in zip(b, z[1:]):
                near.arrive()
                sib.start()

    def finish(self):
        for z in self.z:
            for copy in z:
                copy.arrive()


def reduce_plan(rows, steps):
    plan = []
    for axis, bit in steps:
        halve = axis == "f" or rows % 32 == 0
        rows = rows // 2 if halve else rows
        plan.append((axis, bit, halve, rows))
    return plan


class Reduce:
    def __init__(self, wire, plan, c, f, nf, grad, boxes, steps, result, spread, lsem):
        self.wire, self.plan, self.c, self.f, self.grad, self.boxes, self.steps = wire, plan, c, f, grad, boxes, steps
        self.result, self.spread, self.lsem = result, spread, lsem
        self.base = f * (grad.shape[0] // nf)
        self.rows_us = 2 * 2 * grad.shape[1] / 98e3
        self.step, self.low, self.marks = 0, 0, []

    def peer(self, axis, bit):
        return (self.c, flip(self.f, bit)) if axis == "f" else (flip(self.c, bit), self.f)

    def send(self):
        if self.step == len(self.steps):
            return self.settle()
        axis, bit, halve, n = self.steps[self.step]
        mine = ((self.f if axis == "f" else self.c) // bit) % 2
        give = self.low + (1 - mine) * n if halve else self.low
        self.keep = self.low + mine * n if halve else self.low
        self.moving = self.wire.copy(self.grad.at[span(give, n)], self.boxes[self.step], *self.peer(axis, bit)).start()
        self.plan.later(self.plan.ship(road(axis, bit, n * self.rows_us)), self.add)

    def add(self):
        axis, bit, halve, n = self.steps[self.step]
        self.moving.arrive()
        box, grad, keep = self.boxes[self.step], self.grad, self.keep
        if not halve:
            self.wire.drain([self.moving])
        width = next(w for w in (128, 96, 64, 48, 32, 16) if n % w == 0)

        @pl.loop(0, n // width)
        def _(i):
            rows = span(keep + i * width, width)
            grad[rows, :] = (grad[rows, :].astype(F32) + box[span(i * width, width), :].astype(F32)).astype(BF)

        self.plan.now += n * grad.shape[1] / 4e5
        if axis == "c" and halve:
            self.marks.append((bit, keep, n))
        self.low, self.n = keep, n
        self.step += 1
        self.send()

    def settle(self):
        self.local = pltpu.make_async_copy(self.grad.at[span(self.low, self.n)], self.result(self.low - self.base, self.n), self.lsem)
        self.local.start()
        self.first = True
        self.give_back()

    def give_back(self):
        if self.local and (not self.first or not self.marks):
            self.local.wait()
            self.local = None
        if not self.marks:
            self.spread()
            return
        bit, low, n = self.marks.pop()
        mine = (self.c // bit) % 2
        there = low + n - 2 * n * mine
        src = self.grad.at[span(low, n)] if self.first else self.result(low - self.base, n)
        self.moving = self.wire.copy(src, self.result(low - self.base, n), flip(self.c, bit), landing=self.result(there - self.base, n)).start()
        self.first = False
        self.plan.later(self.plan.ship(road("c", bit, n * self.rows_us)), self.take_back)

    def take_back(self):
        self.moving.arrive()
        self.give_back()


def norm_rows(v):
    cen = v - jnp.mean(v, axis=-1, keepdims=True)
    rstd = lax.rsqrt(jnp.mean(cen * cen, axis=-1, keepdims=True) + EPS)
    return cen * rstd, rstd


def norm_back(grad, hat, rstd, gain):
    scaled = grad * gain
    return rstd * (scaled - jnp.mean(scaled, axis=-1, keepdims=True) - hat * jnp.mean(scaled * hat, axis=-1, keepdims=True))


def split3(v):
    hi = v.astype(BF).astype(F32)
    mid = (v - hi).astype(BF).astype(F32)
    return hi, mid, v - hi - mid


def layer(cfg, *refs):
    nc, nf, p, plans = cfg["nc"], cfg["nf"], cfg["p"], cfg["plans"]
    names = cfg["names"]
    R = dict(zip(names, refs, strict=True))
    x, cot, vec, lens = R["x"], R["cot"], R["vec"], R["lens"]
    wq_s, wo_s, wu_s, wd_s = R["wq_s"], R["wo_s"], R["wu_s"], R["wd_s"]
    wl, wo, wu, wd = R["wl"], R["wo"], R["wu"], R["wd"]
    vsum, bu = R["vsum"], R["bu"]
    xg, h1g, qp, kp, vp, of = R["xg"], R["h1g"], R["qp"], R["kp"], R["vp"], R["of"]
    omsg, oin, o2, res, h2, gb, gh = R["omsg"], R["oin"], R["o2"], R["res"], R["h2"], R["gb"], R["gh"]
    c, f = lax.axis_index("ctx"), lax.axis_index("fsdp")
    qs = nc // GROUPS
    g, m = c // qs, c % qs
    rows, D = x.shape
    T = rows // 2
    FF = wu.shape[1]
    core = c % 2
    sib = flip(c, 1)
    top = g // 4
    gq = g % 4
    odd = (gq % 2) == 1
    gf = flip(g, 4)
    far = flip(c, nc // 2)
    NQ = GROUPS * T
    NK = NQ * qs
    lsem = R["lsem"]
    wire = Wire(R["send"], R["recv"], f)

    done = set()

    def ready(i):
        if i not in done:
            loads[i].wait()
            done.add(i)

    lane = lax.broadcasted_iota(jnp.int32, (T, 128), 1)
    low = lane < HDIM

    off = (3 * (gq // 2) + gq % 2) * 128
    loads = []

    def load(src, dst):
        cp = pltpu.make_async_copy(src, dst, lsem.at[len(loads)])
        cp.start()
        loads.append(cp)

    nq = wq_s.shape[0]
    wcols = [span(i * D + off, 256, 128) for i in range(3)]
    for i in range(3):
        load(wq_s.at[:, wcols[i]], wl.at[span(f * nq, nq), i * 256 : (i + 1) * 256])
    for s, w in ((wo_s, wo), (wu_s, wu), (wd_s, wd)):
        load(s, w.at[span(f * s.shape[0], s.shape[0])])

    barrier = pltpu.get_barrier_semaphore()
    mates = [(((g + k) % GROUPS) * qs + m, f) for k in range(1, GROUPS)]
    mates += [(g * qs + (m + k) % qs, f) for k in range(1, qs)]
    mates += [(c, (f + k) % nf) for k in range(1, nf)]
    for mate in mates:
        pl.semaphore_signal(barrier, inc=1, device_id=mate, device_id_type=MESH)
    pl.semaphore_wait(barrier, len(mates))

    own_rows, other_rows = span(top * T, T), span((1 - top) * T, T)
    to_far = wire.copy(x.at[other_rows], xg.at[g], far, landing=xg.at[gf]).start()
    near = [(top * 4 + (gq + k) % 4, top * 4 + (gq + 4 - k) % 4) for k in (1, 2, 3)]
    own_out = [wire.copy(x.at[own_rows], xg.at[g], t * qs + m, landing=xg.at[s]).start() for t, s in near]
    far_out = [wire.copy(xg.at[gf], xg.at[gf], t * qs + m, landing=xg.at[flip(s, 4)]) for t, s in near]
    wq_out, vec_out = [], []
    for d in range(1, nf):
        fs = (f + nf - d) % nf
        vec_out.append(wire.copy(vec, R["vin"].at[d], c, (f + d) % nf).start())
        for i in range(3):
            cols = slice(i * 256, (i + 1) * 256)
            wq_out.append(wire.copy(wq_s.at[:, wcols[i]], wl.at[span(f * nq, nq), cols], c, (f + d) % nf,
                                    landing=wl.at[span(fs * nq, nq), cols]).start())
    weights = [Gather(wire, c, f, nf, p, s, w) for s, w in ((wo_s, wo), (wu_s, wu), (wd_s, wd))]
    for w in weights:
        w.begin()
    to_far.arrive()
    for copy in far_out:
        copy.start()
    xg[g] = x[own_rows, :]
    for copy in vec_out:
        copy.arrive()
    total = vec[...].astype(F32)
    for d in range(1, nf):
        total = total + R["vin"][d].astype(F32)
    vsum[...] = total
    for i in range(FF // D):
        bu[0:1, i * D : (i + 1) * D] = vsum[8 + i : 9 + i, :]
    for mb in range(2):
        pos = c * T + lax.broadcasted_iota(jnp.int32, (T, D), 0)
        live = pos < lens[mb]
        gb[mb * T : (mb + 1) * T, :] = jnp.where(live, cot[mb * T : (mb + 1) * T, :].astype(F32), 0.0).astype(BF)
    hd = D // 2
    mine, theirs = span(core * hd, hd, 128), span((1 - core) * hd, hd, 128)
    gh[0:rows, :] = gb[:, mine]
    lower, upper = slice(0, rows), slice(rows, 2 * rows)
    g_out = wire.copy(gb.at[:, theirs], gh.at[upper], sib).start()

    for i in range(3):
        ready(i)
    for copy in wq_out:
        copy.arrive()
    length = jnp.where(top == 0, lens[0], lens[1])
    kaug_hi = jnp.where((lane >= 64) & (lane < 68), 1.0, 0.0)
    kaug_lo = jnp.where(lane < 4, 1.0, 0.0)
    vaug_hi = jnp.where((lane >= 64) & (lane < 67), 1.0, 0.0)
    vaug_lo = jnp.where(lane < 3, 1.0, 0.0)
    one_hi, one_lo = jnp.where(lane == 64, 1.0, 0.0), jnp.where(lane == 0, 1.0, 0.0)
    bias_q = vsum[2:3, span(off, 256, 128)]
    bias_v = vsum[3:4, span(off, 256, 128)]

    def pick(t0, t1):
        return jnp.where(odd, t1, t0), jnp.where(odd, pltpu.roll(t0, HDIM, 1), t1)

    def project(s):
        hat, _ = norm_rows(xg[s].astype(F32))
        h1 = (hat * vsum[0:1, :] + vsum[1:2, :]).astype(BF)
        qrows = span(s * T, T, 128)
        krows = span((m * GROUPS + s) * T, T, 128)
        h1g[qrows, :] = h1
        y = dot_nn(h1, wl[...])
        q = y[:, 0:256] + bias_q
        v = y[:, 512:768] + bias_v
        qa, qc = pick(q[:, 0:128], q[:, 128:256])
        ka, kc = pick(y[:, 256:384], y[:, 384:512])
        va, vc = pick(v[:, 0:128], v[:, 128:256])
        pos = (s * qs + m) * T + lax.broadcasted_iota(jnp.int32, (T, 128), 0)
        bias = jnp.where(pos < length, 0.0, -1e30)
        k_hi = jnp.where(lane == 64, bias, kaug_hi)
        k_lo = jnp.where(lane == 0, bias, kaug_lo)
        qa, qc = qa.astype(BF).astype(F32) * 0.125, qc.astype(BF).astype(F32) * 0.125
        qp[0, qrows, :] = jnp.where(low, qa, one_hi).astype(BF)
        qp[1, qrows, :] = jnp.where(low, one_lo, qa).astype(BF)
        qp[2, qrows, :] = jnp.where(low, qc, one_hi).astype(BF)
        kp[0, krows, :] = jnp.where(low, ka, k_hi).astype(BF)
        kp[1, krows, :] = jnp.where(low, k_lo, ka).astype(BF)
        kp[2, krows, :] = jnp.where(low, kc, k_hi).astype(BF)
        vp[0, krows, :] = jnp.where(low, va, vaug_hi).astype(BF)
        vp[1, krows, :] = jnp.where(low, vaug_lo, va).astype(BF)
        vp[2, krows, :] = jnp.where(low, vc, vaug_hi).astype(BF)

    def share(first):
        out = []
        for j in range(1, qs):
            for ref in (kp, vp):
                at = lambda who: ref.at[:, span((who * GROUPS + first) * T, 4 * T, 128), :]
                out.append(wire.copy(at(m), at(m), g * qs + (m + j) % qs, landing=at((m + qs - j) % qs)).start())
        return out

    for copy in own_out:
        copy.arrive()
    pl.loop(0, 4)(lambda i: project(top * 4 + i))
    shares = share(top * 4)
    for copy in far_out:
        copy.arrive()
    pl.loop(0, 4)(lambda i: project((1 - top) * 4 + i))
    shares += share((1 - top) * 4)
    weights[0].spread()
    weights[1].spread()
    for copy in shares:
        copy.arrive()
    weights[2].spread()

    tq = cfg["tq"]
    lane_q = lax.broadcasted_iota(jnp.int32, (tq, 128), 1)

    def attend(h):
        base = 0 if h == 1 else HDIM

        @pl.loop(0, NQ // tq)
        def _(i):
            at = span(i * tq, tq, 128)
            q = qp[h, at, :]
            s = dot_nt(q, kp[h])
            peak = jnp.max(s, axis=1, keepdims=True)
            e = jnp.exp(s - peak).astype(BF)
            o = dot_nn(e, vp[h])
            l = o[:, base : base + 1]
            of[h, at, :] = o / l
            a, b, d = split3(-(peak + jnp.log(l)))
            q = q.astype(F32)
            q = jnp.where(lane_q == base + 1, a, jnp.where(lane_q == base + 2, b, jnp.where(lane_q == base + 3, d, q)))
            qp[h, at, :] = q.astype(BF)

    def deal(msg, box, half):
        box[half, g] = msg[half, g]
        out = []
        for k in range(1, GROUPS):
            t, s = (g + k) % GROUPS, (g + GROUPS - k) % GROUPS
            out.append(wire.copy(msg.at[half, t], box.at[half, g], t * qs + m, landing=box.at[half, s]).start())
        return out

    attend(0)
    attend(1)

    @pl.loop(0, GROUPS)
    def _(s):
        at = span(s * T, T, 128)
        omsg[0, s] = jnp.where(low, of[0, at, :], of[1, at, :]).astype(BF)

    o_out = deal(omsg, oin, 0)
    weights[0].pass_on()
    attend(2)

    @pl.loop(0, GROUPS)
    def _(s):
        omsg[1, s] = of[2, span(s * T, T, 128), :].astype(BF)

    o_out += deal(omsg, oin, 1)
    weights[1].pass_on()
    weights[2].pass_on()
    for copy in o_out:
        copy.arrive()

    def tiles(jp):
        return [slice((3 * jp + i) * 128, (3 * jp + i + 1) * 128) for i in range(3)]

    for mb in range(2):
        for jp in range(2):
            g0 = 4 * mb + 2 * jp
            at = slice(mb * T, (mb + 1) * T)
            t0, t1, t2 = tiles(jp)
            o2[at, t0] = oin[0, g0]
            o2[at, t1] = jnp.where(low, oin[1, g0].astype(F32), pltpu.roll(oin[1, g0 + 1].astype(F32), HDIM, 1)).astype(BF)
            o2[at, t2] = oin[0, g0 + 1]
    o_pair = wire.copy(o2.at[lower], o2.at[upper], sib).start()
    ready(3)
    weights[0].finish()
    res[...] = x[...].astype(F32) + dot_nn(o2[lower, :], wo[...]) + vsum[4:5, :]
    hat2, _ = norm_rows(res[...])
    h2[lower, :] = (hat2 * vsum[5:6, :] + vsum[6:7, :]).astype(BF)
    h_pair = wire.copy(h2.at[lower], h2.at[upper], sib).start()
    for i in (1, 2):
        ready(3 + i)
        weights[i].finish()

    a2, duh, dus, dbu, acc, dh2 = R["a2"], R["duh"], R["dus"], R["dbu"], R["acc"], R["dh2"]
    acc[...] = jnp.zeros_like(acc)
    dh2[...] = jnp.zeros_like(dh2)
    hf = FF // 2

    def hidden(which, keep):
        @pl.loop(0, hf // WIDE)
        def _(i):
            col = which * hf + i * WIDE
            cols = span(col, WIDE, 128)
            u = dot_nn(h2[lower, :], wu[:, cols]) + bu[:, cols]
            phi = 0.5 + 0.5 * lax.erf(u * 0.7071067811865476)
            a = (u * phi).astype(BF)
            a2[lower, cols] = a
            da = dot_nt(gb[...], wd[span(col, WIDE, 128), :])
            slope = phi + u * (0.3989422804014327 * jnp.exp(-0.5 * u * u))
            du = (da * slope).astype(BF)
            keep[0:rows, span(i * WIDE, WIDE, 128)] = du
            dbu[:, cols] = jnp.sum(du.astype(F32), axis=0, keepdims=True)
            acc[...] += dot_nn(a, wd[span(col, WIDE, 128), :])
            dh2[...] += dot_nt(du, wu[:, cols])

    hidden(1 - core, dus)
    du_pair = wire.copy(dus, duh.at[upper], sib).start()
    half_cols = lambda which: span(which * hf, hf, 128)
    a_pair = [wire.copy(a2.at[lower, half_cols(1 - core)], a2.at[upper, half_cols(1 - core)], sib, landing=a2.at[upper, half_cols(core)]).start()]
    hidden(core, duh)
    a_pair.append(wire.copy(a2.at[lower, half_cols(core)], a2.at[upper, half_cols(core)], sib, landing=a2.at[upper, half_cols(1 - core)]).start())
    R["out"][...] = (res[...] + acc[...] + vsum[7:8, :]).astype(BF)
    plan = Planner()
    a_here = plan.ship({"core": 5.0})
    dr, dbh, dbs, dmsg, doin = R["dr"], R["dbh"], R["dbs"], omsg, R["doin"]
    dvb = R["dvb"]
    gd, gu, go, gqr = wd.at[:, 0:hd], wu.at[:, 0:hf], wo.at[:, 0:hd], wu.at[:, hf : hf + D]

    def residual_back():
        hat2, rstd2 = norm_rows(res[...])
        dvb[0, 5:6, :] = jnp.sum(dh2[...] * hat2, axis=0, keepdims=True)
        dvb[0, 6:7, :] = jnp.sum(dh2[...], axis=0, keepdims=True)
        dr[...] = gb[...].astype(F32) + norm_back(dh2[...], hat2, rstd2, vsum[5:6, :])
        db = dr[...].astype(BF)
        dbs[...] = db
        dvb[0, 4:5, :] = jnp.sum(db.astype(F32), axis=0, keepdims=True)
        dvb[0, 7:8, :] = jnp.sum(gb[...].astype(F32), axis=0, keepdims=True)
        dbh[0:rows, :] = dbs[:, mine]
        db_pair = wire.copy(dbs.at[:, theirs], dbh.at[upper], sib).start()
        acc[...] = dot_nt(db, wo[...])
        wire.drain(o_out)
        for t in range(GROUPS):
            mb, jj = t // 4, t % 4
            at = slice(mb * T, (mb + 1) * T)
            t0, t1, t2 = tiles(jj // 2)
            dmsg[0, t] = acc[at, t2 if jj % 2 else t0].astype(BF)
            single = acc[at, t1]
            dmsg[1, t] = (pltpu.roll(single, HDIM, 1) if jj % 2 else single).astype(BF)
        do_out = [deal(dmsg, doin, 0), deal(dmsg, doin, 1)]
        load = {"x": 2.7, "z": 4.0, "mid": 5.4}
        here = [plan.ship(load), plan.ship(load)]
        for w in weights:
            for copies in [w.a] + w.b + w.z:
                wire.drain(copies)
        wire.drain(far_out)
        return db_pair, do_out, here

    db_pair, do_out, do_here = plan.compute(2.0, residual_back)

    def shard(ref, half, c0, c1, lead=()):
        return lambda lo, n: ref.at[lead + (span(lo, n), span(core * half + c0, c1 - c0, 128))]

    lone = []

    def sibling(ref, half, c0, c1):
        def go():
            at = lambda which: ref.at[:, span(which * half + c0, c1 - c0, 128)]
            copy = wire.copy(at(core), at(core), sib, landing=at(1 - core)).start()
            plan.later(plan.ship({"core": 1.0}), copy.arrive)
        return go

    def reduction(k, j, grad, ref, half, c0, c1):
        boxes = [R[f"box_{k}{j}{i}"] for i in range(len(plans[k]))]
        Reduce(wire, plan, c, f, nf, grad.at[:, c0:c1], boxes, plans[k], shard(ref, half, c0, c1), sibling(ref, half, c0, c1),
               lsem.at[7 + len(lone)]).send()
        lone.append(k)

    def down_grads():
        for copy in a_pair:
            copy.arrive()
        g_out.arrive()

        @pl.loop(0, FF // WIDE)
        def _(i):
            at = span(i * WIDE, WIDE, 128)
            wd[at, 0:hd] = dot_tn(a2[:, at], gh[...]).astype(BF)

        for j, (c0, c1) in enumerate(cfg["cuts"]["d"]):
            reduction("d", j, gd, R["fd"], hd, c0, c1)

    plan.compute(2.0, down_grads, a_here)

    def up_grads():
        h_pair.arrive()
        du_pair.arrive()
        for j, (c0, c1) in enumerate(cfg["cuts"]["u"]):
            wu[:, c0:c1] = dot_tn(h2[...], duh[:, c0:c1]).astype(BF)
            reduction("u", j, gu, R["fu"], hf, c0, c1)

    plan.compute(2.2, up_grads)

    def out_grads():
        o_pair.arrive()
        db_pair.arrive()
        wo[:, 0:hd] = dot_tn(o2[...], dbh[...]).astype(BF)
        for j, (c0, c1) in enumerate(cfg["cuts"]["o"]):
            reduction("o", j, go, R["fo"], hd, c0, c1)

    plan.compute(0.7, out_grads)

    dop, dka, dva, dkv, dkvin, dqkv = (R[k] for k in ("dop", "dka", "dva", "dkv", "dkvin", "dqkv"))
    dqa = of
    tb, kc = cfg["tb"], cfg["kc"]
    lane_b = lax.broadcasted_iota(jnp.int32, (tb, 128), 1)

    def prepare(h):
        half = 1 if h == 2 else 0
        base = 0 if h == 1 else HDIM

        @pl.loop(0, GROUPS)
        def _(s):
            at = span(s * T, T, 128)
            d = doin[half, s].astype(F32)
            d = jnp.where(low, 0.0, d) if h == 1 else jnp.where(low, d, 0.0)
            a, b, e = split3(-jnp.sum(d * of[h, at, :], axis=1, keepdims=True))
            d = jnp.where(lane == base, a, jnp.where(lane == base + 1, b, jnp.where(lane == base + 2, e, d)))
            dop[h, at, :] = d.astype(BF)

    def retrace(h, first, last):
        keep = (lambda v: jnp.where(lane_b < HDIM, 0.0, v)) if h == 1 else (lambda v: jnp.where(lane_b < HDIM, v, 0.0))
        if h != 1 and first == 0:
            dka[...] = jnp.zeros((NK, 128), F32)
            dva[...] = jnp.zeros((NK, 128), F32)

        @pl.loop(first, last)
        def _(i):
            at = span(i * tb, tb, 128)
            q, d = qp[h, at, :], dop[h, at, :]
            q0, d0 = keep(q.astype(F32)).astype(BF), keep(d.astype(F32)).astype(BF)
            dq = jnp.zeros((tb, 128), F32)
            for j in range(NK // kc):
                ks = slice(j * kc, (j + 1) * kc)
                k, v = kp[h, ks, :], vp[h, ks, :]
                pt = jnp.exp(dot_nt(k, q))
                ds = (pt * dot_nt(v, d)).astype(BF)
                dva[ks, :] += dot_nn(pt.astype(BF), d0)
                dka[ks, :] += dot_nn(ds, q0)
                dq = dq + dot_tn(ds, k)
            dqa[h, at, :] = dq * 0.125

    def trade(half):
        out = []
        for j in range(1, qs):
            part = (m + j) % qs

            @pl.loop(0, GROUPS)
            def _(s):
                at = span((part * GROUPS + s) * T, T, 128)
                to = span(s * T, T, 128)
                dkv[j - 1, 0, to, :] = dka[at, :].astype(BF)
                dkv[j - 1, 1, to, :] = dva[at, :].astype(BF)

            out.append(wire.copy(dkv.at[j - 1], dkvin.at[j - 1, half], g * qs + part).start())
        return out

    def place(half, base, at, tile):
        if half == 0:
            dqkv[at, base : base + 128] = jnp.where(odd, dqkv[at, base : base + 128].astype(F32), tile).astype(BF)
            dqkv[at, base + 128 : base + 256] = jnp.where(odd, tile, dqkv[at, base + 128 : base + 256].astype(F32)).astype(BF)
        else:
            turned = pltpu.roll(tile, HDIM, 1)
            dqkv[at, base : base + 128] = jnp.where(odd, turned, dqkv[at, base : base + 128].astype(F32)).astype(BF)
            dqkv[at, base + 128 : base + 256] = jnp.where(odd, dqkv[at, base + 128 : base + 256].astype(F32), tile).astype(BF)

    def settle_heads(half, trades):
        for copy in trades:
            copy.arrive()
        wire.drain(trades)
        pair = half == 0

        @pl.loop(0, GROUPS)
        def _(s):
            at = span(s * T, T, 128)
            mine_at = span((m * GROUPS + s) * T, T, 128)
            if pair:
                tile = jnp.where(low, dqa[0, at, :], dqa[1, at, :])
            else:
                tile = jnp.where(low, dqa[2, at, :], 0.0)
            place(half, 0, at, tile)
            for which, acc_ref in ((0, dka), (1, dva)):
                tile = acc_ref[mine_at, :]
                for j in range(1, qs):
                    tile = tile + dkvin[j - 1, half, which, at, :].astype(F32)
                place(half, 256 * (which + 1), at, tile)

    def retrace_all(h):
        n = NQ // tb
        for first, last in ((0, n // 2), (n // 2, n)):
            plan.compute(3.2, lambda: retrace(h, first, last))

    def ready_pair():
        dqkv[...] = jnp.zeros_like(dqkv)
        for copy in do_out[0]:
            copy.arrive()
        prepare(0)
        prepare(1)

    def ready_single():
        for copy in do_out[1]:
            copy.arrive()
        prepare(2)

    plan.compute(1.9, ready_pair, do_here[0])
    retrace_all(0)
    retrace_all(1)
    trades = plan.compute(0.5, lambda: trade(0))
    pair_here = plan.ship({"core": 3.0})
    plan.compute(1.0, ready_single, do_here[1])
    plan.compute(1.0, lambda: settle_heads(0, trades), pair_here)
    retrace_all(2)
    trades = plan.compute(0.5, lambda: trade(1))
    plan.compute(1.0, lambda: settle_heads(1, trades), plan.ship({"core": 3.0}))

    dh1p, dh1in, dh1, farbox = xg, R["dh1in"], dh2, R["farbox"]
    gqh, box_c = wu.at[:, hf + D : hf + D + hd], R["box_c"]

    def inputs_back():
        pl.loop(0, GROUPS)(lambda s: dh1p.__setitem__(s, dot_nt(dqkv[span(s * T, T, 128), :], wl[...]).astype(BF)))
        out = [wire.copy(dh1p.at[flip(t, 4)], dh1in.at[k, 1], t * qs + m).start() for k, (t, s) in enumerate(near)]
        out += [wire.copy(dh1p.at[t], dh1in.at[k, 0], t * qs + m).start() for k, (t, s) in enumerate(near)]
        return out

    dh_out = plan.compute(2.0, inputs_back)
    dh_here = [plan.ship({"x": 8.0, "z": 8.0}), plan.ship({"x": 8.0, "z": 8.0})]

    def qkv_grads():
        for i in range(0, D, 256):
            gqr[:, i : i + 256] = dot_tn(h1g[...], dqkv[:, i : i + 256]).astype(BF)
        return wire.copy(gqr.at[:, theirs], box_c, sib).start()

    gq_pair = plan.compute(2.0, qkv_grads)
    gq_here = plan.ship({"core": 2.0})

    def column_sums():
        colsum = lax.fori_loop(
            0, GROUPS, lambda i, t: t + jnp.sum(dqkv[span(i * T, T, 128), :].astype(F32), axis=0, keepdims=True), jnp.zeros((1, D), F32)
        )
        dvb[0, 2:4, :] = jnp.zeros((2, D), F32)
        dvb[0, 12:16, :] = jnp.zeros((4, D), F32)
        dvb[0, 2:3, span(off, 256, 128)] = colsum[:, 0:256]
        dvb[0, 3:4, span(off, 256, 128)] = colsum[:, 512:768]
        for i in range(FF // D):
            dvb[0, 8 + i : 9 + i, :] = dbu[0:1, i * D : (i + 1) * D]

    plan.compute(0.5, column_sums)
    fq = R["fq"]

    def spread_q():
        moves = [(2, [gq]), (1, [gq, flip(gq, 2)]), (0, None)]

        def go():
            bit, have = moves.pop(0)
            if bit:
                ref = lambda jj: fq.at[jj, :, span(core * hd, hd, 128)]
                mate = flip(c, bit * qs)
                copies = [wire.copy(ref(j), ref(j), mate, landing=ref(flip(j, bit))).start() for j in have]
                us = len(have) * fq.shape[1] * hd * 4 / 98e3
            else:
                at = lambda which: fq.at[:, :, span(which * hd, hd, 128)]
                copies = [wire.copy(at(core), at(core), sib, landing=at(1 - core)).start()]
                us = 12.0

            def come():
                for copy in copies:
                    copy.arrive()
                if moves:
                    go()

            plan.later(plan.ship(road("c", 2 * bit if bit else 1, us)), come)

        go()

    def sum_q():
        gq_pair.arrive()
        gqh[...] = (gqr[:, mine].astype(F32) + box_c[...].astype(F32)).astype(BF)
        Reduce(wire, plan, c, f, nf, gqh, [R[f"box_q0{i}"] for i in range(len(plans["q"]))], plans["q"],
               shard(fq, hd, 0, hd, (gq,)), spread_q, lsem.at[6]).send()

    plan.compute(0.5, sum_q, gq_here)

    def total_of(which, block):
        s = dh1p[block].astype(F32)
        for k in range(3):
            s = s + dh1in[k, which].astype(F32)
        return s

    def far_total():
        for copy in dh_out[:3]:
            copy.arrive()
        farbox[0] = total_of(1, gf).astype(BF)
        return wire.copy(farbox.at[0], farbox.at[1], far).start()

    far_back = plan.compute(0.5, far_total, dh_here[0])
    far_here = plan.ship({"z": 4.0, "mid": 8.0})

    def near_total():
        for copy in dh_out[3:]:
            copy.arrive()
        dh1[own_rows, :] = total_of(0, g)

    plan.compute(0.5, near_total, dh_here[1])
    dvin = R["dvin"]
    bits = [("c", 1 << b) for b in range(nc.bit_length() - 1)] + [("f", 1 << b) for b in range(nf.bit_length() - 1)]

    def vectors(i=0):
        if i == len(bits):
            R["dvec"][...] = dvb[i]
            return
        axis, bit = bits[i]
        peer = (c, flip(f, bit)) if axis == "f" else (flip(c, bit), f)
        moved = wire.copy(dvb.at[i], dvin.at[i], *peer).start()

        def come():
            moved.arrive()
            dvb[i + 1] = dvb[i] + dvin[i]
            vectors(i + 1)

        plan.later(plan.ship(road(axis, bit, 1.0)), come)

    def finish_inputs():
        far_back.arrive()
        dh1[other_rows, :] = farbox[1].astype(F32)
        hat1, rstd1 = norm_rows(x[...].astype(F32))
        dvb[0, 0:1, :] = jnp.sum(dh1[...] * hat1, axis=0, keepdims=True)
        dvb[0, 1:2, :] = jnp.sum(dh1[...], axis=0, keepdims=True)
        vectors()
        R["gin"][...] = (dr[...] + norm_back(dh1[...], hat1, rstd1, vsum[0:1, :])).astype(BF)

    plan.compute(1.7, finish_inputs, far_here)
    plan.finish()
    wire.drain()


def call(nc, nf, x, cot, vec, lens, wq, wo, wu, wd):
    qs = nc // GROUPS
    R, D = x.shape
    T, FF = R // 2, wu.shape[1]
    NQ, NK = GROUPS * T, GROUPS * T * qs
    hd, hf = D // 2, FF // 2
    p = next(p for p in (8, 4, 2) if nc % p == 0 and all(w.shape[0] % (16 * p) == 0 for w in (wo, wu, wd)))
    fbits = [("f", 1 << b) for b in reversed(range(nf.bit_length() - 1))]
    cbits = [("c", 1 << b) for b in range(1, nc.bit_length() - 1)]
    qbits = [("c", 1 << b) for b in range(1, qs.bit_length() - 1)] + [("c", nc // 2)]
    plans = {"d": reduce_plan(FF, fbits + cbits), "u": reduce_plan(D, fbits + cbits), "o": reduce_plan(D, fbits + cbits),
             "q": reduce_plan(D, fbits + qbits)}
    sds, dma = jax.ShapeDtypeStruct, pltpu.SemaphoreType.DMA
    any_, vm, sm = (pl.BlockSpec(memory_space=s) for s in (pl.ANY, pltpu.VMEM, pltpu.SMEM))
    ins = ["x", "cot", "vec", "lens", "wq_s", "wo_s", "wu_s", "wd_s"]
    outs = {"out": sds((R, D), BF), "gin": sds((R, D), BF), "dvec": sds((16, D), F32), "fq": sds((4, D // nf, D), BF),
            "fo": sds((D // nf, D), BF), "fu": sds((D // nf, FF), BF), "fd": sds((FF // nf, D), BF)}
    nb = nc.bit_length() + nf.bit_length() - 2
    b, s = (lambda *shape: pltpu.VMEM(shape, BF)), (lambda *shape: pltpu.VMEM(shape, F32))
    scratch = {
        "wl": b(D, D), "wo": b(D, D), "wu": b(D, FF), "wd": b(FF, D), "vsum": s(16, D), "bu": s(1, FF), "vin": b(nf, 16, D),
        "xg": b(GROUPS, T, D), "h1g": b(NQ, D), "qp": b(3, NQ, 128), "kp": b(3, NK, 128), "vp": b(3, NK, 128), "of": s(3, NQ, 128),
        "omsg": b(2, GROUPS, T, 128), "oin": b(2, GROUPS, T, 128), "o2": b(2 * R, D), "res": s(R, D), "h2": b(2 * R, D), "gb": b(R, D),
        "gh": b(2 * R, hd), "a2": b(2 * R, FF), "duh": b(2 * R, hf), "dus": b(R, hf), "dbu": s(1, FF), "acc": s(R, D), "dh2": s(R, D),
        "dr": s(R, D), "dbh": b(2 * R, hd), "dbs": b(R, D), "doin": b(2, GROUPS, T, 128),
        "dop": b(3, NQ, 128), "dka": s(NK, 128), "dva": s(NK, 128),
        "dkv": b(qs - 1, 2, NQ, 128), "dkvin": b(qs - 1, 2, 2, NQ, 128), "dqkv": b(NQ, D),
        "dh1in": b(3, 2, T, D), "farbox": b(2, T, D),
        "box_c": b(D, hd), "dvb": s(nb + 1, 16, D), "dvin": s(nb, 16, D),
        "lsem": dma((16,)), "send": dma((400,)), "recv": dma((400,)),
    }
    cuts = {"d": [(i, i + 128) for i in range(0, hd, 128)], "u": [(i, i + 512) for i in range(0, hf, 512)], "o": [(0, hd)], "q": [(0, hd)]}
    for k in cuts:
        for j, (c0, c1) in enumerate(cuts[k]):
            for i, (_, _, _, n) in enumerate(plans[k]):
                scratch[f"box_{k}{j}{i}"] = b(n, c1 - c0)
    cfg = dict(nc=nc, nf=nf, p=p, plans=plans, names=ins + list(outs) + list(scratch), cuts=cuts, tq=128, tb=256, kc=512)
    return pl.pallas_call(
        functools.partial(layer, cfg),
        out_shape=list(outs.values()),
        in_specs=[vm, vm, vm, sm, any_, any_, any_, any_],
        out_specs=[vm, vm, vm, any_, any_, any_, any_],
        scratch_shapes=list(scratch.values()),
        compiler_params=pltpu.CompilerParams(collective_id=0, has_side_effects=True, vmem_limit_bytes=62_464 * 1024),
    )(x, cot, vec, lens, wq, wo, wu, wd)


def body(inputs, cotangent, lengths, g1, b1, w_qkv, bias_q, bias_v, w_out, bias_out, g2, b2, w_up, bias_up, w_down, bias_down, nc, nf):
    MB, _, T, D = inputs.shape
    f = lax.axis_index("fsdp")
    small = [g1, b1, bias_q, bias_v, bias_out, g2, b2, bias_down, bias_up]
    flat = jnp.concatenate([jnp.tile(v, nf) for v in small])
    owner = jnp.concatenate([jnp.repeat(jnp.arange(nf), v.shape[0]) for v in small])
    vec = jnp.where(owner == f, flat, 0).astype(BF).reshape(-1, D)
    vec = jnp.pad(vec, ((0, 16 - vec.shape[0]), (0, 0)))
    out, gin, dvec, fq, fo, fu, fd = call(nc, nf, inputs.reshape(MB * T, D), cotangent.reshape(MB * T, D), vec, lengths[:, 0],
                                          w_qkv, w_out, w_up, w_down)
    n = g1.shape[0]
    row = lambda i: lax.dynamic_slice(dvec[i], (f * n,), (n,))
    up = lax.dynamic_slice(dvec[8:12].reshape(-1), (f * bias_up.shape[0],), bias_up.shape)
    parts = fq.astype(F32)
    cols = []
    for t in range(3):
        for a in range(2):
            x0, x1 = parts[2 * a, :, 256 * t : 256 * t + 256], parts[2 * a + 1, :, 256 * t : 256 * t + 256]
            cols += [x0[:, :128], x0[:, 128:] + x1[:, :128], x1[:, 128:]]
    shape = (MB, 1, T, D)
    return (out.reshape(shape), gin.reshape(shape), row(0), row(1), jnp.concatenate(cols, axis=1), row(2), row(3), fo.astype(F32), row(4),
            row(5), row(6), fu.astype(F32), up, fd.astype(F32), row(7))


def solution(mesh):
    nc, nf = mesh.shape["ctx"], mesh.shape["fsdp"]
    act = P(None, "fsdp", "ctx", None)
    one, two = P("fsdp"), P("fsdp", None)
    return jax.shard_map(
        functools.partial(body, nc=nc, nf=nf),
        mesh=mesh,
        in_specs=(act, act, P(None, "fsdp"), one, one, two, one, one, two, one, one, one, two, one, two, one),
        out_specs=(act, act, one, one, two, one, one, two, one, one, one, two, one, two, one),
        check_vma=False,
    )
```

time: 1290 us -> 252 us (0.20)
  waiting for transfers between devices: 881 us -> 0 us
  Pallas kernels: 0 us -> 226 us
  matrix products: 169 us -> 0 us
  blocking collectives: 90.3 us -> 0 us
  local copies, waits for them, and re-layouts: 65.8 us -> 16 us
  other arithmetic: 55.7 us -> 8.6 us
  between operations: 17.6 us -> 0.99 us
    reduce_scatter x8 -> x0, waiting for transfers between devices: 375 us -> none  [the longest x2 122 us: body(): lax.psum_scatter(local_grads[11].astype(jnp.bfloat16), 'fsdp', scatter_di...]
    all_gather x8 -> x0, waiting for transfers between devices: 271 us -> none  [the longest x2 79.2 us: body(): piece_values = lax.all_gather(value_rows, 'ctx', axis=0, tiled=True)]
    pallas_call x0 -> x1, Pallas kernels: none -> 226 us  [call(): pl.pallas_call(functools.partial(layer, cfg), out_shape=list(outs.values(...]
    dot_general x36 -> x0, matrix products: 169 us -> none  [the longest x2 21.1 us: body(): jnp.einsum('qhd,khd->hqk', split_heads(grad_attended), split_heads(back_p...]
    unnamed x25 -> x0, waiting for transfers between devices: 161 us -> none
    psum x1 -> x0, waiting for transfers between devices: 73.7 us -> none  [body(): lax.psum(for_sending(totals), 'ctx')]
    psum x1 -> x0, blocking collectives: 54.7 us -> none  [body(): lax.psum(for_sending(totals), 'ctx')]
    all_gather x9 -> x0, blocking collectives: 29.5 us -> none  [the longest x1 3.55 us: body(): lax.all_gather(bias_up, 'fsdp', axis=0, tiled=True)]
  transfers between devices with their start and end apart: 21 -> 0, of which waited for: 20 -> 0; matrix products, arithmetic and copies ran while one was open for 18% -> 0% of each run, Pallas kernels for 0% -> 0%
where the time goes in v1:
time: 252 us
  Pallas kernels  226 us (90%)
  local copies, waits for them, and re-layouts  16 us (6%)
  other arithmetic  8.6 us (3%)
    pallas_call x1, Pallas kernels, call(): pl.pallas_call(functools.partial(layer, cfg), out_shape=list(outs.values(...  226 us
    another operation x18, local copies, waits for them, and re-layouts, body(): flat = jnp.concatenate([jnp.tile(v, nf) for v in small])  6.32 us
    unnamed x43, local copies, waits for them, and re-layouts  5.35 us

profile of v1, /device:TPU:3, one launch (start us, length us, event | category | flops | bytes accessed | tf_op | source)
XLA Modules:
  0.0 251.9 jit_solution(9496987983714089416)
XLA Ops:
  0.8 0.7 tile.36
  1.8 0.7 tile.38
  2.7 0.7 tile.40
  3.6 0.7 tile.42
  4.6 0.7 tile.44
  5.5 0.7 tile.91
  6.4 0.7 tile.93
  7.4 0.7 tile.95
  8.3 0.7 tile.97
  9.1 0.6 pad.4.refs_2_
  9.7 226.2 %shard_map.271 = (bf16[256,768]{1,0:T(8,128)(2,1)}, bf16[256,768]{1,0:T(8,128)(2,1)}, f32[16,768]{1,0:T(8,128)}, bf16[4,384,768]{2,1,0:T(8,128)(2,1)}, bf16[384,...) custom-call(bf16[256,768]{1,0:T(8,128)(2,1)} %bitcast.33, bf16[256,768]{1,0:T(8,128)(2,1)} %bitcast.34, ...), custom_call_target="tpu_custom_call" | custom-call | tf_op jit(solution)/shard_map/pallas_call | solution.py:887
  235.9 2.1 convert_element_type.16
  238.0 0.5 slice_bitcast_fusion
  239.0 1.8 copy-done.6
  240.8 0.6 fusion.8
  241.4 0.6 fusion.10
  242.0 0.6 fusion.12
  242.7 0.6 fusion.6
  243.3 0.7 dynamic_slice.57
  244.0 2.8 %convert_element_type.18 = f32[384,3072]{1,0:T(8,128)} convert(bf16[384,3072]{1,0:T(8,128)(2,1)S(1)} %copy-done.1) | non-fusion elementwise | flops 1179648 | bytes 7077888 | tf_op jit(solution)/shard_map/convert_element_type | solution.py:918
  246.7 2.5 %convert_element_type.19 = f32[1536,768]{1,0:T(8,128)} convert(bf16[1536,768]{1,0:T(8,128)(2,1)S(1)} %copy-done) | non-fusion elementwise | flops 1179648 | bytes 7077888 | tf_op jit(solution)/shard_map/convert_element_type | solution.py:918
  249.3 1.1 convert_element_type.17
  250.4 0.7 copy.70
  251.1 0.7 copy.71
  (69 shorter events, 2.5 us)
Async XLA Ops:
  238.6 2.2 copy-start.5
  238.6 5.3 %copy-start.1 = (bf16[384,3072]{1,0:T(8,128)(2,1)S(1)}, bf16[384,3072]{1,0:T(8,128)(2,1)}, u32[]{:S(2)}) copy-start(bf16[384,3072]{1,0:T(8,128)(2,1)} %get-tuple-element.27) | copy-start | bytes 7077892
  239.0 1.8 copy-start.6
  244.0 2.8 %copy-start = (bf16[1536,768]{1,0:T(8,128)(2,1)S(1)}, bf16[1536,768]{1,0:T(8,128)(2,1)}, u32[]{:S(2)}) copy-start(bf16[1536,768]{1,0:T(8,128)(2,1)} %get-tuple-element.28) | copy-start | bytes 7077892
  246.7 2.6 %copy-start.2 = (bf16[384,768]{1,0:T(8,128)(2,1)S(1)}, bf16[384,768]{1,0:T(8,128)(2,1)}, u32[]{:S(2)}) copy-start(bf16[384,768]{1,0:T(8,128)(2,1)} %get-tuple-element.26) | copy-start | bytes 1769476
  246.7 3.6 %copy-start.4 = (bf16[256,768]{1,0:T(8,128)(2,1)S(1)}, bf16[256,768]{1,0:T(8,128)(2,1)}, u32[]{:S(2)}) copy-start(bf16[256,768]{1,0:T(8,128)(2,1)} %get-tuple-element.22) | copy-start | bytes 1179652
  246.7 4.4 %copy-start.3 = (bf16[256,768]{1,0:T(8,128)(2,1)S(1)}, bf16[256,768]{1,0:T(8,128)(2,1)}, u32[]{:S(2)}) copy-start(bf16[256,768]{1,0:T(8,128)(2,1)} %get-tuple-element.23) | copy-start | bytes 1179652

commit v2 on v1

--- a/solution.py
+++ b/solution.py
@@ -329,7 +329,7 @@
     wq_out, vec_out = [], []
     for d in range(1, nf):
         fs = (f + nf - d) % nf
-        vec_out.append(wire.copy(vec, R["vin"].at[d], c, (f + d) % nf).start())
+        vec_out.append(wire.copy(vec, R["vin"].at[f], c, (f + d) % nf, landing=R["vin"].at[fs]).start())
         for i in range(3):
             cols = slice(i * 256, (i + 1) * 256)
             wq_out.append(wire.copy(wq_s.at[:, wcols[i]], wl.at[span(f * nq, nq), cols], c, (f + d) % nf,
@@ -341,14 +341,13 @@
     for copy in far_out:
         copy.start()
     xg[g] = x[own_rows, :]
+    vin = R["vin"]
+    vin[f] = vec[...]
     for copy in vec_out:
         copy.arrive()
-    total = vec[...].astype(F32)
-    for d in range(1, nf):
-        total = total + R["vin"][d].astype(F32)
-    vsum[...] = total
-    for i in range(FF // D):
-        bu[0:1, i * D : (i + 1) * D] = vsum[8 + i : 9 + i, :]
+    vsum[...] = jnp.concatenate([vin[j].astype(F32) for j in range(nf)], axis=1)
+    nv = vec.shape[1]
+    bu[...] = jnp.concatenate([vsum[8 + i : 9 + i, j * nv : (j + 1) * nv] for j in range(nf) for i in range(FF // D)], axis=1)
     for mb in range(2):
         pos = c * T + lax.broadcasted_iota(jnp.int32, (T, D), 0)
         live = pos < lens[mb]
@@ -728,7 +727,7 @@
     plan.compute(1.0, lambda: settle_heads(1, trades), plan.ship({"core": 3.0}))
 
     dh1p, dh1in, dh1, farbox = xg, R["dh1in"], dh2, R["farbox"]
-    gqh, box_c = wu.at[:, hf + D : hf + D + hd], R["box_c"]
+    gqh, box_c = wu.at[:, hf + D : hf + D + hd], dop
 
     def inputs_back():
         pl.loop(0, GROUPS)(lambda s: dh1p.__setitem__(s, dot_nt(dqkv[span(s * T, T, 128), :], wl[...]).astype(BF)))
@@ -742,7 +741,9 @@
     def qkv_grads():
         for i in range(0, D, 256):
             gqr[:, i : i + 256] = dot_tn(h1g[...], dqkv[:, i : i + 256]).astype(BF)
-        return wire.copy(gqr.at[:, theirs], box_c, sib).start()
+        return [
+            wire.copy(gqr.at[:, span((1 - core) * hd + i * 128, 128, 128)], box_c.at[i, 0:D], sib).start() for i in range(hd // 128)
+        ]
 
     gq_pair = plan.compute(2.0, qkv_grads)
     gq_here = plan.ship({"core": 2.0})
@@ -787,8 +788,11 @@
         go()
 
     def sum_q():
-        gq_pair.arrive()
-        gqh[...] = (gqr[:, mine].astype(F32) + box_c[...].astype(F32)).astype(BF)
+        for copy in gq_pair:
+            copy.arrive()
+        for i in range(hd // 128):
+            at = slice(i * 128, (i + 1) * 128)
+            gqh[:, at] = (gqr[:, span(core * hd + i * 128, 128, 128)].astype(F32) + box_c[i, 0:D].astype(F32)).astype(BF)
         Reduce(wire, plan, c, f, nf, gqh, [R[f"box_q0{i}"] for i in range(len(plans["q"]))], plans["q"],
                shard(fq, hd, 0, hd, (gq,)), spread_q, lsem.at[6]).send()
 
@@ -803,8 +807,9 @@
     def far_total():
         for copy in dh_out[:3]:
             copy.arrive()
-        farbox[0] = total_of(1, gf).astype(BF)
-        return wire.copy(farbox.at[0], farbox.at[1], far).start()
+        wire.drain([g_out])
+        gb[0:T, :] = total_of(1, gf).astype(BF)
+        return wire.copy(gb.at[0:T], farbox, far).start()
 
     far_back = plan.compute(0.5, far_total, dh_here[0])
     far_here = plan.ship({"z": 4.0, "mid": 8.0})
@@ -820,7 +825,16 @@
 
     def vectors(i=0):
         if i == len(bits):
-            R["dvec"][...] = dvb[i]
+            final, own = dvb[i], jnp.zeros((16, nv), F32)
+            for j in range(nf):
+                own = jnp.where(f == j, final[:, j * nv : (j + 1) * nv], own)
+            for r in range(FF // D):
+                for j in range(nf):
+                    flat = (j * (FF // D) + r) * nv
+                    piece = final[8 + flat // D : 9 + flat // D, flat % D : flat % D + nv]
+                    R["dvec"][8 + r : 9 + r, :] = piece if j == 0 else jnp.where(f == j, piece, R["dvec"][8 + r : 9 + r, :])
+            R["dvec"][0:8, :] = own[0:8]
+            R["dvec"][12:16, :] = own[12:16]
             return
         axis, bit = bits[i]
         peer = (c, flip(f, bit)) if axis == "f" else (flip(c, bit), f)
@@ -835,7 +849,7 @@
 
     def finish_inputs():
         far_back.arrive()
-        dh1[other_rows, :] = farbox[1].astype(F32)
+        dh1[other_rows, :] = farbox[...].astype(F32)
         hat1, rstd1 = norm_rows(x[...].astype(F32))
         dvb[0, 0:1, :] = jnp.sum(dh1[...] * hat1, axis=0, keepdims=True)
         dvb[0, 1:2, :] = jnp.sum(dh1[...], axis=0, keepdims=True)
@@ -844,6 +858,21 @@
 
     plan.compute(1.7, finish_inputs, far_here)
     plan.finish()
+    gq_o = R["gq"]
+    nrow = fq.shape[1]
+    step = next(n for n in (128, 96, 64, 48, 32, 16) if nrow % n == 0)
+
+    @pl.loop(0, nrow // step)
+    def _(i):
+        at = span(i * step, step)
+        for t in range(3):
+            for a in range(2):
+                base, src = t * D + a * 384, 256 * t
+                gq_o[at, base : base + 128] = fq[2 * a, at, src : src + 128]
+                shared = fq[2 * a, at, src + 128 : src + 256].astype(F32) + fq[2 * a + 1, at, src : src + 128].astype(F32)
+                gq_o[at, base + 128 : base + 256] = shared.astype(BF)
+                gq_o[at, base + 256 : base + 384] = fq[2 * a + 1, at, src + 128 : src + 256]
+
     wire.drain()
 
 
@@ -862,20 +891,21 @@
     sds, dma = jax.ShapeDtypeStruct, pltpu.SemaphoreType.DMA
     any_, vm, sm = (pl.BlockSpec(memory_space=s) for s in (pl.ANY, pltpu.VMEM, pltpu.SMEM))
     ins = ["x", "cot", "vec", "lens", "wq_s", "wo_s", "wu_s", "wd_s"]
-    outs = {"out": sds((R, D), BF), "gin": sds((R, D), BF), "dvec": sds((16, D), F32), "fq": sds((4, D // nf, D), BF),
+    outs = {"out": sds((R, D), BF), "gin": sds((R, D), BF), "dvec": sds((16, D // nf), F32), "gq": sds((D // nf, 3 * D), BF),
             "fo": sds((D // nf, D), BF), "fu": sds((D // nf, FF), BF), "fd": sds((FF // nf, D), BF)}
     nb = nc.bit_length() + nf.bit_length() - 2
     b, s = (lambda *shape: pltpu.VMEM(shape, BF)), (lambda *shape: pltpu.VMEM(shape, F32))
     scratch = {
-        "wl": b(D, D), "wo": b(D, D), "wu": b(D, FF), "wd": b(FF, D), "vsum": s(16, D), "bu": s(1, FF), "vin": b(nf, 16, D),
+        "wl": b(D, D), "wo": b(D, D), "wu": b(D, FF), "wd": b(FF, D), "vsum": s(16, D), "bu": s(1, FF), "vin": b(nf, 16, D // nf),
         "xg": b(GROUPS, T, D), "h1g": b(NQ, D), "qp": b(3, NQ, 128), "kp": b(3, NK, 128), "vp": b(3, NK, 128), "of": s(3, NQ, 128),
         "omsg": b(2, GROUPS, T, 128), "oin": b(2, GROUPS, T, 128), "o2": b(2 * R, D), "res": s(R, D), "h2": b(2 * R, D), "gb": b(R, D),
         "gh": b(2 * R, hd), "a2": b(2 * R, FF), "duh": b(2 * R, hf), "dus": b(R, hf), "dbu": s(1, FF), "acc": s(R, D), "dh2": s(R, D),
         "dr": s(R, D), "dbh": b(2 * R, hd), "dbs": b(R, D), "doin": b(2, GROUPS, T, 128),
         "dop": b(3, NQ, 128), "dka": s(NK, 128), "dva": s(NK, 128),
         "dkv": b(qs - 1, 2, NQ, 128), "dkvin": b(qs - 1, 2, 2, NQ, 128), "dqkv": b(NQ, D),
-        "dh1in": b(3, 2, T, D), "farbox": b(2, T, D),
-        "box_c": b(D, hd), "dvb": s(nb + 1, 16, D), "dvin": s(nb, 16, D),
+        "dh1in": b(3, 2, T, D), "farbox": b(T, D),
+        "dvb": s(nb + 1, 16, D), "dvin": s(nb, 16, D),
+        "fq": b(4, D // nf, D),
         "lsem": dma((16,)), "send": dma((400,)), "recv": dma((400,)),
     }
     cuts = {"d": [(i, i + 128) for i in range(0, hd, 128)], "u": [(i, i + 512) for i in range(0, hf, 512)], "o": [(0, hd)], "q": [(0, hd)]}
@@ -888,7 +918,7 @@
         functools.partial(layer, cfg),
         out_shape=list(outs.values()),
         in_specs=[vm, vm, vm, sm, any_, any_, any_, any_],
-        out_specs=[vm, vm, vm, any_, any_, any_, any_],
+        out_specs=[vm, vm, vm, vm, any_, any_, any_],
         scratch_shapes=list(scratch.values()),
         compiler_params=pltpu.CompilerParams(collective_id=0, has_side_effects=True, vmem_limit_bytes=62_464 * 1024),
     )(x, cot, vec, lens, wq, wo, wu, wd)
@@ -896,26 +926,19 @@
 
 def body(inputs, cotangent, lengths, g1, b1, w_qkv, bias_q, bias_v, w_out, bias_out, g2, b2, w_up, bias_up, w_down, bias_down, nc, nf):
     MB, _, T, D = inputs.shape
-    f = lax.axis_index("fsdp")
-    small = [g1, b1, bias_q, bias_v, bias_out, g2, b2, bias_down, bias_up]
-    flat = jnp.concatenate([jnp.tile(v, nf) for v in small])
-    owner = jnp.concatenate([jnp.repeat(jnp.arange(nf), v.shape[0]) for v in small])
-    vec = jnp.where(owner == f, flat, 0).astype(BF).reshape(-1, D)
-    vec = jnp.pad(vec, ((0, 16 - vec.shape[0]), (0, 0)))
+    n = g1.shape[0]
+    small, at, flat = [g1, b1, bias_q, bias_v, bias_out, g2, b2, bias_down, bias_up], 0, 0
+    for v in small:
+        flat = flat + lax.pad(v, jnp.zeros((), BF), ((at, 16 * n - at - v.shape[0], 0),))
+        at += v.shape[0]
+    vec = flat.reshape(16, n)
     out, gin, dvec, fq, fo, fu, fd = call(nc, nf, inputs.reshape(MB * T, D), cotangent.reshape(MB * T, D), vec, lengths[:, 0],
                                           w_qkv, w_out, w_up, w_down)
-    n = g1.shape[0]
-    row = lambda i: lax.dynamic_slice(dvec[i], (f * n,), (n,))
-    up = lax.dynamic_slice(dvec[8:12].reshape(-1), (f * bias_up.shape[0],), bias_up.shape)
-    parts = fq.astype(F32)
-    cols = []
-    for t in range(3):
-        for a in range(2):
-            x0, x1 = parts[2 * a, :, 256 * t : 256 * t + 256], parts[2 * a + 1, :, 256 * t : 256 * t + 256]
-            cols += [x0[:, :128], x0[:, 128:] + x1[:, :128], x1[:, 128:]]
+    grads = [v.astype(F32) for v in (fq, fo, fu, fd)]
     shape = (MB, 1, T, D)
-    return (out.reshape(shape), gin.reshape(shape), row(0), row(1), jnp.concatenate(cols, axis=1), row(2), row(3), fo.astype(F32), row(4),
-            row(5), row(6), fu.astype(F32), up, fd.astype(F32), row(7))
+    row = lambda i: dvec[i]
+    return (out.reshape(shape), gin.reshape(shape), row(0), row(1), grads[0], row(2), row(3), grads[1], row(4),
+            row(5), row(6), grads[2], dvec[8:12].reshape(-1), grads[3], row(7))
 
 
 def solution(mesh):

time: 252 us -> 243 us (0.964)
  local copies, waits for them, and re-layouts: 16 us -> 5.08 us
    another operation x18 -> x0, local copies, waits for them, and re-layouts: 6.32 us -> none  [body(): flat = jnp.concatenate([jnp.tile(v, nf) for v in small])]
    unnamed x43 -> x12, local copies, waits for them, and re-layouts: 5.35 us -> 1.51 us
    dynamic_slice x5 -> x0, local copies, waits for them, and re-layouts: 3.09 us -> none  [the longest x4 2.41 us: body(): row = lambda i: lax.dynamic_slice(dvec[i], (f * n,), (n,))]
where the time goes in v2:
time: 243 us; the launch traced here: 242 us
  Pallas kernels  226 us (93%)
  other arithmetic  11.1 us (5%)
  local copies, waits for them, and re-layouts  5.08 us (2%)
    pallas_call x1, Pallas kernels, call(): pl.pallas_call(functools.partial(layer, cfg), out_shape=list(outs.values(...  226 us
    convert_element_type x4, other arithmetic, body(): grads = [v.astype(F32) for v in (fq, fo, fu, fd)]  10.2 us

profile of v2, /device:TPU:3, one launch (start us, length us, event | category | flops | bytes accessed | tf_op | source)
XLA Modules:
  0.0 242.3 jit_solution(11488806447710938211)
XLA Ops:
  0.6 0.8 pad_add_fusion
  1.5 0.6 reshape.50.refs_2_
  2.1 225.5 %shard_map.271 = (bf16[256,768]{1,0:T(8,128)(2,1)}, bf16[256,768]{1,0:T(8,128)(2,1)}, f32[16,384]{1,0:T(8,128)}, bf16[384,2304]{1,0:T(8,128)(2,1)}, bf16[384,768...) custom-call(bf16[256,768]{1,0:T(8,128)(2,1)} %bitcast.9, bf16[256,768]{1,0:T(8,128)(2,1)} %bitcast.10, ...), custom_call_target="tpu_custom_call" | custom-call | tf_op jit(solution)/shard_map/pallas_call | solution.py:917
  227.6 1.6 slice_reduce_fusion
  229.3 0.7 slice.34
  230.0 0.6 reshape.53
  230.6 0.0 copy-start
  230.6 4.6 %convert_element_type.14 = f32[384,3072]{1,0:T(8,128)} convert(bf16[384,3072]{1,0:T(8,128)(2,1)} %get-tuple-element.27) | non-fusion elementwise | flops 1179648 | bytes 7077888 | tf_op jit(solution)/shard_map/convert_element_type | solution.py:937
  235.2 0.0 copy-done
  235.2 0.0 copy-start.1
  235.2 2.5 %convert_element_type.15 = f32[1536,768]{1,0:T(8,128)} convert(bf16[1536,768]{1,0:T(8,128)(2,1)S(1)} %copy-done) | non-fusion elementwise | flops 1179648 | bytes 7077888 | tf_op jit(solution)/shard_map/convert_element_type | solution.py:937
  237.7 0.0 copy-done.1
  237.7 0.0 copy-start.2
  237.7 0.0 copy-start.4
  237.7 2.0 convert_element_type.12
  239.7 0.0 copy-start.3
  239.7 0.0 copy-done.2
  239.7 1.1 convert_element_type.13
  240.8 0.0 copy-done.4
  240.8 0.7 copy.35
  241.6 0.0 copy-done.3
  241.6 0.7 copy.36
Async XLA Ops:
  230.6 4.6 %copy-start = (bf16[1536,768]{1,0:T(8,128)(2,1)S(1)}, bf16[1536,768]{1,0:T(8,128)(2,1)}, u32[]{:S(2)}) copy-start(bf16[1536,768]{1,0:T(8,128)(2,1)} %get-tuple-element.28) | copy-start | bytes 7077892
  235.2 2.5 %copy-start.1 = (bf16[384,2304]{1,0:T(8,128)(2,1)S(1)}, bf16[384,2304]{1,0:T(8,128)(2,1)}, u32[]{:S(2)}) copy-start(bf16[384,2304]{1,0:T(8,128)(2,1)} %get-tuple-element.25) | copy-start | bytes 5308420
  237.7 2.0 copy-start.2
  237.7 3.1 %copy-start.4 = (bf16[256,768]{1,0:T(8,128)(2,1)S(1)}, bf16[256,768]{1,0:T(8,128)(2,1)}, u32[]{:S(2)}) copy-start(bf16[256,768]{1,0:T(8,128)(2,1)} %get-tuple-element.22) | copy-start | bytes 1179652
  239.7 1.8 copy-start.3

commit v3 on v2

--- a/solution.py
+++ b/solution.py
@@ -334,7 +334,7 @@
             cols = slice(i * 256, (i + 1) * 256)
             wq_out.append(wire.copy(wq_s.at[:, wcols[i]], wl.at[span(f * nq, nq), cols], c, (f + d) % nf,
                                     landing=wl.at[span(fs * nq, nq), cols]).start())
-    weights = [Gather(wire, c, f, nf, p, s, w) for s, w in ((wo_s, wo), (wu_s, wu), (wd_s, wd))]
+    weights = [Gather(wire, c, f, nf, n, s, w) for n, s, w in ((p, wo_s, wo), (p, wu_s, wu), (min(p, 4), wd_s, wd))]
     for w in weights:
         w.begin()
     to_far.arrive()

time: 243 us -> 238 us (0.979)
  Pallas kernels: 226 us -> 220 us
    pallas_call x1, Pallas kernels: 226 us -> 220 us  [call(): pl.pallas_call(functools.partial(layer, cfg), out_shape=list(outs.values(...]
where the time goes in v3:
time: 238 us; the launch traced here: 237 us
  Pallas kernels  220 us (92%)
  other arithmetic  11.1 us (5%)
  local copies, waits for them, and re-layouts  5.08 us (2%)
    pallas_call x1, Pallas kernels, call(): pl.pallas_call(functools.partial(layer, cfg), out_shape=list(outs.values(...  220 us
    convert_element_type x4, other arithmetic, body(): grads = [v.astype(F32) for v in (fq, fo, fu, fd)]  10.2 us

profile of v3, /device:TPU:3, one launch (start us, length us, event | category | flops | bytes accessed | tf_op | source)
XLA Modules:
  0.0 237.2 jit_solution(18380180569317426145)
XLA Ops:
  0.6 0.8 pad_add_fusion
  1.5 0.6 reshape.50.refs_2_
  2.1 220.4 %shard_map.271 = (bf16[256,768]{1,0:T(8,128)(2,1)}, bf16[256,768]{1,0:T(8,128)(2,1)}, f32[16,384]{1,0:T(8,128)}, bf16[384,2304]{1,0:T(8,128)(2,1)}, bf16[384,768...) custom-call(bf16[256,768]{1,0:T(8,128)(2,1)} %bitcast.9, bf16[256,768]{1,0:T(8,128)(2,1)} %bitcast.10, ...), custom_call_target="tpu_custom_call" | custom-call | tf_op jit(solution)/shard_map/pallas_call | solution.py:917
  222.5 1.6 slice_reduce_fusion
  224.2 0.7 slice.34
  224.9 0.6 reshape.53
  225.5 0.0 copy-start
  225.5 4.6 %convert_element_type.14 = f32[384,3072]{1,0:T(8,128)} convert(bf16[384,3072]{1,0:T(8,128)(2,1)} %get-tuple-element.27) | non-fusion elementwise | flops 1179648 | bytes 7077888 | tf_op jit(solution)/shard_map/convert_element_type | solution.py:937
  230.0 0.0 copy-done
  230.0 0.0 copy-start.1
  230.0 2.5 %convert_element_type.15 = f32[1536,768]{1,0:T(8,128)} convert(bf16[1536,768]{1,0:T(8,128)(2,1)S(1)} %copy-done) | non-fusion elementwise | flops 1179648 | bytes 7077888 | tf_op jit(solution)/shard_map/convert_element_type | solution.py:937
  232.6 0.0 copy-done.1
  232.6 0.0 copy-start.2
  232.6 0.0 copy-start.4
  232.6 2.0 convert_element_type.12
  234.6 0.0 copy-start.3
  234.6 0.0 copy-done.2
  234.6 1.1 convert_element_type.13
  235.7 0.0 copy-done.4
  235.7 0.7 copy.35
  236.5 0.0 copy-done.3
  236.5 0.7 copy.36
Async XLA Ops:
  225.5 4.6 %copy-start = (bf16[1536,768]{1,0:T(8,128)(2,1)S(1)}, bf16[1536,768]{1,0:T(8,128)(2,1)}, u32[]{:S(2)}) copy-start(bf16[1536,768]{1,0:T(8,128)(2,1)} %get-tuple-element.28) | copy-start | bytes 7077892
  230.0 2.5 %copy-start.1 = (bf16[384,2304]{1,0:T(8,128)(2,1)S(1)}, bf16[384,2304]{1,0:T(8,128)(2,1)}, u32[]{:S(2)}) copy-start(bf16[384,2304]{1,0:T(8,128)(2,1)} %get-tuple-element.25) | copy-start | bytes 5308420
  232.6 2.0 copy-start.2
  232.6 3.1 %copy-start.4 = (bf16[256,768]{1,0:T(8,128)(2,1)S(1)}, bf16[256,768]{1,0:T(8,128)(2,1)}, u32[]{:S(2)}) copy-start(bf16[256,768]{1,0:T(8,128)(2,1)} %get-tuple-element.22) | copy-start | bytes 1179652
  234.6 1.8 copy-start.3

commit v4 on v3

--- a/solution.py
+++ b/solution.py
@@ -334,7 +334,7 @@
             cols = slice(i * 256, (i + 1) * 256)
             wq_out.append(wire.copy(wq_s.at[:, wcols[i]], wl.at[span(f * nq, nq), cols], c, (f + d) % nf,
                                     landing=wl.at[span(fs * nq, nq), cols]).start())
-    weights = [Gather(wire, c, f, nf, n, s, w) for n, s, w in ((p, wo_s, wo), (p, wu_s, wu), (min(p, 4), wd_s, wd))]
+    weights = [Gather(wire, c, f, nf, n, s, w) for n, s, w in ((p, wo_s, wo), (min(p, 4), wu_s, wu), (min(p, 4), wd_s, wd))]
     for w in weights:
         w.begin()
     to_far.arrive()

time: 238 us -> 246 us (1.034)
  Pallas kernels: 220 us -> 229 us
    pallas_call x1, Pallas kernels: 220 us -> 229 us  [call(): pl.pallas_call(functools.partial(layer, cfg), out_shape=list(outs.values(...]
where the time goes in v4:
time: 246 us
  Pallas kernels  229 us (93%)
  other arithmetic  11.1 us (5%)
  local copies, waits for them, and re-layouts  5.08 us (2%)
    pallas_call x1, Pallas kernels, call(): pl.pallas_call(functools.partial(layer, cfg), out_shape=list(outs.values(...  229 us
    convert_element_type x4, other arithmetic, body(): grads = [v.astype(F32) for v in (fq, fo, fu, fd)]  10.2 us

profile of v4, /device:TPU:3, one launch (start us, length us, event | category | flops | bytes accessed | tf_op | source)
XLA Modules:
  0.0 245.7 jit_solution(8801531681032131258)
XLA Ops:
  0.6 0.8 pad_add_fusion
  1.5 0.6 reshape.50.refs_2_
  2.1 228.9 %shard_map.271 = (bf16[256,768]{1,0:T(8,128)(2,1)}, bf16[256,768]{1,0:T(8,128)(2,1)}, f32[16,384]{1,0:T(8,128)}, bf16[384,2304]{1,0:T(8,128)(2,1)}, bf16[384,768...) custom-call(bf16[256,768]{1,0:T(8,128)(2,1)} %bitcast.9, bf16[256,768]{1,0:T(8,128)(2,1)} %bitcast.10, ...), custom_call_target="tpu_custom_call" | custom-call | tf_op jit(solution)/shard_map/pallas_call | solution.py:917
  231.0 1.6 slice_reduce_fusion
  232.6 0.7 slice.34
  233.3 0.6 reshape.53
  233.9 0.0 copy-start
  233.9 4.6 %convert_element_type.14 = f32[384,3072]{1,0:T(8,128)} convert(bf16[384,3072]{1,0:T(8,128)(2,1)} %get-tuple-element.27) | non-fusion elementwise | flops 1179648 | bytes 7077888 | tf_op jit(solution)/shard_map/convert_element_type | solution.py:937
  238.5 0.0 copy-done
  238.5 0.0 copy-start.1
  238.5 2.5 %convert_element_type.15 = f32[1536,768]{1,0:T(8,128)} convert(bf16[1536,768]{1,0:T(8,128)(2,1)S(1)} %copy-done) | non-fusion elementwise | flops 1179648 | bytes 7077888 | tf_op jit(solution)/shard_map/convert_element_type | solution.py:937
  241.0 0.0 copy-done.1
  241.0 0.0 copy-start.2
  241.0 0.0 copy-start.4
  241.0 2.0 convert_element_type.12
  243.1 0.0 copy-start.3
  243.1 0.0 copy-done.2
  243.1 1.1 convert_element_type.13
  244.2 0.0 copy-done.4
  244.2 0.7 copy.35
  244.9 0.0 copy-done.3
  244.9 0.7 copy.36
Async XLA Ops:
  233.9 4.6 %copy-start = (bf16[1536,768]{1,0:T(8,128)(2,1)S(1)}, bf16[1536,768]{1,0:T(8,128)(2,1)}, u32[]{:S(2)}) copy-start(bf16[1536,768]{1,0:T(8,128)(2,1)} %get-tuple-element.28) | copy-start | bytes 7077892
  238.5 2.5 %copy-start.1 = (bf16[384,2304]{1,0:T(8,128)(2,1)S(1)}, bf16[384,2304]{1,0:T(8,128)(2,1)}, u32[]{:S(2)}) copy-start(bf16[384,2304]{1,0:T(8,128)(2,1)} %get-tuple-element.25) | copy-start | bytes 5308420
  241.0 2.0 copy-start.2
  241.0 3.1 %copy-start.4 = (bf16[256,768]{1,0:T(8,128)(2,1)S(1)}, bf16[256,768]{1,0:T(8,128)(2,1)}, u32[]{:S(2)}) copy-start(bf16[256,768]{1,0:T(8,128)(2,1)} %get-tuple-element.22) | copy-start | bytes 1179652
  243.1 1.8 copy-start.3
